TPU v7x, 512 devices: a whole 4x4x16 slice. The times are simulated.
512 devices in a mesh: group: 16 (over x, y_hi, core), tensor: 32 (over z, y_lo).
Axes of the slice: x: 4, y: 4 (y_hi: 2, y_lo: 2; y = y_hi * 2 + y_lo), z: 16, core: 2. Of those that a mesh axis runs over, the one named last changes fastest.
Arguments:
- x_prompt: bfloat16 [2048, 16384], P('group', 'tensor'), may hold values from -6 to 6
- z_prompt: bfloat16 [2048, 16384], P('group', 'tensor'), may hold values from -6 to 6
- conv_weight: bfloat16 [4, 16384], P(None, 'tensor'), may hold values from -3 to 3
- conv_bias: bfloat16 [16384], P('tensor'), may hold values from -0.5 to 0.5
- xproj_weight: bfloat16 [16384, 544], P('tensor'), may hold values from -0.046875 to 0.046875
- dtproj_weight: bfloat16 [512, 16384], P(None, 'tensor'), may hold values from -0.25 to 0.25
- dt_bias: float32 [16384], P('tensor'), may hold values from -7 to -2.5
- decay_rate: float32 [16384, 16], P('tensor'), may hold values from 0.5 to 16
- skip_gain: float32 [16384], P('tensor'), may hold values from 0.5 to 1.5
- sample_prompt: int32 [32], P('group'), may hold values from 0 to 1, as said below
- decode_x: bfloat16 [4, 32, 16384], P(None, 'group', 'tensor'), may hold values from -6 to 6
- decode_z: bfloat16 [4, 32, 16384], P(None, 'group', 'tensor'), may hold values from -6 to 6
Outputs:
- prompt_out: bfloat16 [2048, 16384], P('group', 'tensor')
- decode_out: bfloat16 [4, 32, 16384], P(None, 'group', 'tensor')
Inputs may be any that keep to these rules, and one draw needn't show every extreme that they name: `sample_prompt`: every prompt is continued by exactly 16 samples.
All inputs are finite; a program needn't handle non-finite values.
Results may differ from a plain program's by a relative error of at most 0.013.
Values may be sent and summed in bfloat16 or wider, within the bound.
No kernel may reach another device: no remote copies, remote signals or barrier semaphores. Data moves between devices by JAX's collectives and lax.ppermute only.
A program may use at most 64 MiB of HBM per device.

v0:
```python
import jax
import jax.numpy as jnp
from jax import lax
from jax.sharding import PartitionSpec as P

N = 16
R = 512
STEPS = 4


def passed_along(value, axis, steps):
    count = lax.axis_size(axis)
    first, last = (max(0, -steps), min(count, count - steps))
    return lax.ppermute(value, axis, [(source, source + steps) for source in range(first, last)])


def entering(array, axis, combine, identity):
    peers, mine = (lax.axis_size(axis), lax.axis_index(axis))
    everything = jax.tree.map(
        lambda part, kind: lax.all_gather(part.astype(kind), axis),
        array,
        (jnp.bfloat16, jnp.bfloat16),
    )
    start = jax.tree.map(
        lambda part, zero: jnp.broadcast_to(jnp.asarray(zero, part.dtype), part.shape),
        array,
        identity,
    )

    def lap(k, before):
        reached = k < mine
        new = combine(
            before, jax.tree.map(lambda part, own: part[k].astype(own.dtype), everything, array)
        )
        return jax.tree.map(lambda a, b: jnp.where(reached, a, b), new, before)

    return lax.fori_loop(0, peers, lap, start)


def compose(earlier, later):
    return (earlier[0] * later[0], later[0] * earlier[1] + later[1])


def local_scan(step, rate, inputs, coef_b, coef_c):
    rows, width = step.shape
    block_rows = 32
    count = rows // block_rows

    def local_one_block(state, pieces):
        dt_b, u_b, b_b, c_b = pieces
        decay = jnp.exp(dt_b[:, :, None] * rate[None])
        drive = (dt_b * u_b)[:, :, None] * b_b[:, None, :]
        cum_decay, cum_drive = lax.associative_scan(compose, (decay, drive), axis=0)
        states = cum_decay * state[None] + cum_drive
        values = jnp.einsum("tcn,tn->tc", states, c_b, precision=lax.Precision.HIGHEST)
        return (states[-1], values)

    pieces = (
        step.reshape(count, block_rows, width),
        inputs.reshape(count, block_rows, width),
        coef_b.reshape(count, block_rows, -1),
        coef_c.reshape(count, block_rows, -1),
    )
    end_state, values = lax.scan(
        local_one_block, jnp.zeros((width, rate.shape[1]), jnp.float32), pieces
    )
    return (values.reshape(rows, width), end_state)


def state_reach(step, rate, coef_c, incoming):
    rows, width = step.shape
    block_rows = 32
    count = rows // block_rows

    def state_one_block(prefix, pieces):
        dt_b, c_b = pieces
        reach = prefix[None] + jnp.cumsum(dt_b, 0)
        factor = jnp.exp(reach[:, :, None] * rate[None]) * incoming[None]
        return (reach[-1], jnp.einsum("tcn,tn->tc", factor, c_b, precision=lax.Precision.HIGHEST))

    pieces = (step.reshape(count, block_rows, width), coef_c.reshape(count, block_rows, -1))
    total, values = lax.scan(state_one_block, jnp.zeros((width,), jnp.float32), pieces)
    return (values.reshape(rows, width), total)


def local(
    x_prompt,
    z_prompt,
    conv_weight,
    conv_bias,
    xproj_weight,
    dtproj_weight,
    dt_bias,
    decay_rate,
    skip_gain,
    sample_prompt,
    decode_x,
    decode_z,
):
    rows, width = x_prompt.shape
    taps = conv_weight.shape[0]
    split = lax.axis_size("group") // 2
    rate = -decay_rate
    kernel = conv_weight.astype(jnp.float32)
    offset = conv_bias.astype(jnp.float32)
    place = lax.axis_index("group")
    position = place % split
    rim = passed_along(x_prompt[rows - (taps - 1) :], "group", 1)
    rim = jnp.where(position == 0, jnp.zeros_like(rim), rim)
    extended = jnp.concatenate([rim, x_prompt], 0).astype(jnp.float32)
    mixed = offset[None]
    for k in range(taps):
        mixed = mixed + kernel[k][None] * extended[k : k + rows]
    conv_in = jax.nn.silu(mixed).astype(jnp.bfloat16)
    partial_proj = jnp.dot(conv_in, xproj_weight, preferred_element_type=jnp.float32)
    proj = lax.psum(partial_proj, "tensor")
    dt_low = proj[:, :R].astype(jnp.bfloat16)
    coef_b = proj[:, R : R + N]
    coef_c = proj[:, R + N :]
    step = jax.nn.softplus(
        jnp.dot(dt_low, dtproj_weight, preferred_element_type=jnp.float32) + dt_bias[None]
    )
    inputs = conv_in.astype(jnp.float32)
    local_y, end_state = local_scan(step, rate, inputs, coef_b, coef_c)
    total_step = jnp.sum(step, 0)
    aggregate = jnp.exp(total_step[:, None] * rate)
    tail = x_prompt[rows - (taps - 1) :].astype(jnp.float32)
    last = position == split - 1
    samples = sample_prompt.shape[0]
    send_a = jnp.where(last, jnp.zeros_like(aggregate), aggregate)
    send_b = jnp.where(last, jnp.zeros_like(end_state), end_state)
    carried = entering(
        (send_a, send_b), "group", compose, (jnp.ones_like(aggregate), jnp.zeros_like(end_state))
    )
    incoming = carried[1]
    final_state = aggregate * incoming + end_state
    empty = (
        jnp.zeros((samples, width, N), jnp.float32),
        jnp.zeros((samples, taps - 1, width), jnp.float32),
    )
    states = lax.all_gather(final_state[None], "group", axis=0, tiled=True)
    tails = lax.all_gather(tail[None], "group", axis=0, tiled=True)
    owner = jnp.arange(states.shape[0], dtype=jnp.int32)
    chosen = (
        (owner % split == split - 1)[None, :]
        & (sample_prompt[:, None] == (owner // split)[None, :])
    ).astype(jnp.float32)
    forked_state = empty[0] + jnp.einsum(
        "sr,rcn->scn", chosen, states, precision=lax.Precision.HIGHEST
    )
    forked_tail = jnp.einsum("sr,rkc->skc", chosen, tails, precision=lax.Precision.HIGHEST)
    reach_y, unused_total = state_reach(step, rate, coef_c, incoming)
    result = (local_y + reach_y + skip_gain[None] * inputs) * jax.nn.silu(
        z_prompt.astype(jnp.float32)
    )
    prompt_out = result.astype(jnp.bfloat16)
    window = jnp.concatenate(
        [forked_tail, jnp.transpose(decode_x.astype(jnp.float32), (1, 0, 2))], 1
    )
    dec_list = []
    for step_index in range(STEPS):
        mixed = offset[None]
        for k in range(taps):
            mixed = mixed + kernel[k][None] * window[:, step_index + k]
        dec_list.append(jax.nn.silu(mixed).astype(jnp.bfloat16))
    dec_inputs = jnp.stack(dec_list, 0)
    state = forked_state
    results = []
    for step_index in range(STEPS):
        dec_in = dec_inputs[step_index]
        dec_proj = lax.psum(
            jnp.dot(dec_in, xproj_weight, preferred_element_type=jnp.float32), "tensor"
        )
        dec_low = dec_proj[:, :R].astype(jnp.bfloat16)
        dec_b = dec_proj[:, R : R + N]
        dec_c = dec_proj[:, R + N :]
        dec_step = jax.nn.softplus(
            jnp.dot(dec_low, dtproj_weight, preferred_element_type=jnp.float32) + dt_bias[None]
        )
        dec_f = dec_in.astype(jnp.float32)
        state = (
            jnp.exp(dec_step[:, :, None] * rate[None]) * state
            + (dec_step * dec_f)[:, :, None] * dec_b[:, None, :]
        )
        value = (
            jnp.einsum("scn,sn->sc", state, dec_c, precision=lax.Precision.HIGHEST)
            + skip_gain[None] * dec_f
        )
        results.append(
            (value * jax.nn.silu(decode_z[step_index].astype(jnp.float32))).astype(jnp.bfloat16)
        )
    return (prompt_out, jnp.stack(results, 0))


def solution(mesh):
    placed = (
        P("group", "tensor"),
        P("group", "tensor"),
        P(None, "tensor"),
        P("tensor"),
        P("tensor", None),
        P(None, "tensor"),
        P("tensor"),
        P("tensor", None),
        P("tensor"),
        P("group"),
        P(None, "group", "tensor"),
        P(None, "group", "tensor"),
    )
    return jax.shard_map(
        local,
        mesh=mesh,
        in_specs=placed,
        out_specs=(P("group", "tensor"), P(None, "group", "tensor")),
        check_vma=False,
    )
```

profile of v0, /device:TPU:1, one launch (start us, length us, event | category | flops | bytes accessed | tf_op | source)
XLA Modules:
  0.0 865.7 jit_solution(11865899986213588275)
XLA Ops:
  8.0 6.3 collective-permute-start
  15.1 21.7 %all-gather.4 = f32[16,3,512]{2,1,0:T(4,128)S(1)} all-gather(f32[1,3,512]{2,1,0:T(4,128)S(1)} %get-tuple-element.351), channel_id=4, replica_groups=mesh['group'=16,'tensor'=32] {'group'}, dimensions={0}, use_global_device_ids=true | all-gather | bytes 104448 | tf_op jit(solution)/shard_map/all_gather | solution.py:142
  38.2 100.2 %all-reduce.20 = (f32[2,544]{1,0:T(2,128)S(1)}, f32[2,544]{1,0:T(2,128)S(1)}, f32[2,544]{1,0:T(2,128)S(1)}, f32[2,544]{1,0:T(2,128)S(1)}) all-reduce(f32[2,544]{1,0:T(2,128)S(1)} %fusion.93, f32[2,544]{1,0:T(2,128)S(1)} %fusion.90, f32[2,544]{1,0:T(2,128)S(1)} %fusion.91, ...), channel_id=1, replica_groups=mesh['group'=16,'tensor'=32] {'tensor'}, use_global_device_ids=true, to_apply=%region_12.13 | all-reduce | flops 4352 | bytes 34816 | tf_op jit(solution)/shard_map/psum | solution.py:171
  148.1 249.9 %all-reduce.23.cloned.1.call-done = f32[128,544]{0,1:T(8,128)} async-done(((f32[128,544]{0,1:T(8,128)}), f32[128,544]{0,1:T(8,128)}) %all-reduce.23.cloned.1.call-update) | async-done | bytes 278544 | tf_op jit(solution)/shard_map/psum | solution.py:116
  402.3 352.3 %while.38 = (s32[]{:T(128)}, f32[512,16]{0,1:T(8,128)}, f32[4,32,512]{2,1,0:T(8,128)}, f32[4,32,512]{2,1,0:T(8,128)S(1)}, f32[512,16]{0,1:T(8,128)S(1)}, /*index...) while((s32[]{:T(128)}, f32[512,16]{0,1:T(8,128)}, ...), condition=%wide.region_2.3_spmd, body=%wide.region_1.2_spmd.sunk | while | flops 7544834 | bytes 69489584 | solution.py:64
  454.6 9.2 %pad.198 = f32[32,512,16]{1,2,0:T(8,128)} pad(f32[16,512,16]{1,2,0:T(8,128)} %pad_maximum_fusion.23, f32[]{:T(128)} %constant.112.clone.1..sunk), padding=0_1_1x0_0_0x0_0_0 | pad | bytes 1572868 | tf_op jit(solution)/shard_map/while/body/eval_jaxpr/pad | solution.py:53
  464.7 9.2 %pad.199 = f32[32,512,16]{1,2,0:T(8,128)} pad(f32[16,512,16]{1,2,0:T(8,128)} %add.771, f32[]{:T(128)} %constant.112.clone.1..sunk), padding=1_0_1x0_0_0x0_0_0 | pad | bytes 1572868 | tf_op jit(solution)/shard_map/while/body/eval_jaxpr/pad | solution.py:53
  473.9 5.9 pad.200
  479.9 5.9 pad.201
  542.7 9.2 %pad.198 = f32[32,512,16]{1,2,0:T(8,128)} pad(f32[16,512,16]{1,2,0:T(8,128)} %pad_maximum_fusion.23, f32[]{:T(128)} %constant.112.clone.1..sunk), padding=0_1_1x0_0_0x0_0_0 | pad | bytes 1572868 | tf_op jit(solution)/shard_map/while/body/eval_jaxpr/pad | solution.py:53
  552.8 9.2 %pad.199 = f32[32,512,16]{1,2,0:T(8,128)} pad(f32[16,512,16]{1,2,0:T(8,128)} %add.771, f32[]{:T(128)} %constant.112.clone.1..sunk), padding=1_0_1x0_0_0x0_0_0 | pad | bytes 1572868 | tf_op jit(solution)/shard_map/while/body/eval_jaxpr/pad | solution.py:53
  562.0 5.9 pad.200
  568.0 5.9 pad.201
  630.8 9.2 %pad.198 = f32[32,512,16]{1,2,0:T(8,128)} pad(f32[16,512,16]{1,2,0:T(8,128)} %pad_maximum_fusion.23, f32[]{:T(128)} %constant.112.clone.1..sunk), padding=0_1_1x0_0_0x0_0_0 | pad | bytes 1572868 | tf_op jit(solution)/shard_map/while/body/eval_jaxpr/pad | solution.py:53
  640.8 9.2 %pad.199 = f32[32,512,16]{1,2,0:T(8,128)} pad(f32[16,512,16]{1,2,0:T(8,128)} %add.771, f32[]{:T(128)} %constant.112.clone.1..sunk), padding=1_0_1x0_0_0x0_0_0 | pad | bytes 1572868 | tf_op jit(solution)/shard_map/while/body/eval_jaxpr/pad | solution.py:53
  650.1 5.9 pad.200
  656.0 5.9 pad.201
  718.8 9.2 %pad.198 = f32[32,512,16]{1,2,0:T(8,128)} pad(f32[16,512,16]{1,2,0:T(8,128)} %pad_maximum_fusion.23, f32[]{:T(128)} %constant.112.clone.1..sunk), padding=0_1_1x0_0_0x0_0_0 | pad | bytes 1572868 | tf_op jit(solution)/shard_map/while/body/eval_jaxpr/pad | solution.py:53
  728.9 9.2 %pad.199 = f32[32,512,16]{1,2,0:T(8,128)} pad(f32[16,512,16]{1,2,0:T(8,128)} %add.771, f32[]{:T(128)} %constant.112.clone.1..sunk), padding=1_0_1x0_0_0x0_0_0 | pad | bytes 1572868 | tf_op jit(solution)/shard_map/while/body/eval_jaxpr/pad | solution.py:53
  738.1 5.9 pad.200
  744.1 5.9 pad.201
  754.5 48.7 %all-gather = bf16[8192,16]{0,1:T(8,128)(2,1)S(1)} all-gather(bf16[512,16]{0,1:T(8,128)(2,1)} %get-tuple-element.356), channel_id=2, replica_groups=mesh['group'=16,'tensor'=32] {'group'}, dimensions={0}, use_global_device_ids=true | all-gather | bytes 278528 | tf_op jit(solution)/shard_map/all_gather | solution.py:20
  804.0 20.0 %all-gather.1 = bf16[8192,16]{0,1:T(8,128)(2,1)S(1)} all-gather(bf16[512,16]{0,1:T(8,128)(2,1)S(1)} %select_convert_fusion), channel_id=3, replica_groups=mesh['group'=16,'tensor'=32] {'group'}, dimensions={0}, use_global_device_ids=true | all-gather | bytes 278528 | tf_op jit(solution)/shard_map/all_gather | solution.py:20
  830.0 23.7 %all-gather.3 = f32[8192,16]{0,1:T(8,128)S(1)} all-gather(f32[512,16]{0,1:T(8,128)S(1)} %multiply_add_fusion.3), channel_id=5, replica_groups=mesh['group'=16,'tensor'=32] {'group'}, dimensions={0}, use_global_device_ids=true | all-gather | bytes 557056 | tf_op jit(solution)/shard_map/all_gather | solution.py:141
  (638 shorter events, 263.7 us)
Async XLA Ops:
  7.2 29.9 %copy-start = (bf16[512,544]{0,1:T(8,128)(2,1)S(1)}, bf16[512,544]{0,1:T(8,128)(2,1)}, u32[]{:S(2)}) copy-start(bf16[512,544]{0,1:T(8,128)(2,1)} %param.22) | copy-start | bytes 1671172
  7.2 390.8 %all-reduce.23.cloned.1.call-start = ((), (), s32[]{:S(2)}) async-start(), calls=%async_computation | async-start | bytes 557056 | tf_op jit(solution)/shard_map/psum | solution.py:116
  8.0 133.4 %collective-permute-start = (bf16[3,512]{1,0:T(4,128)(2,1)S(1)}, bf16[3,512]{1,0:T(4,128)(2,1)S(1)}, u32[]{:S(2)}, u32[]{:S(2)}) collective-permute-start(bf16[3,512]{1,0:T(4,128)(2,1)S(1)} %get-tuple-element.352), channel_id=1, source_target_pairs={{0,32},{32,64},{64,96},{96,128},{128,160},{160,192},{192,224},{224... | collective-permute-start | bytes 9224 | tf_op jit(solution)/shard_map/ppermute | solution.py:14
  14.3 22.5 %copy-start.77 = (pred[16]{0:T(512)(128)(4,1)}, pred[16]{0:T(512)(128)(4,1)S(1)}, u32[]{:S(2)}) copy-start(pred[16]{0:T(512)(128)(4,1)S(1)} %fusion.75) | copy-start | bytes 52
  14.4 22.5 %copy-start.79 = (s32[16]{0:T(128)}, s32[16]{0:T(128)S(1)}, u32[]{:S(2)}) copy-start(s32[16]{0:T(128)S(1)} %and_select_fusion) | copy-start | bytes 196
  15.1 131.5 %copy-start.39 = (f32[1,512]{1,0:T(1,128)}, f32[1,512]{1,0:T(1,128)S(1)}, u32[]{:S(2)}) copy-start(f32[1,512]{1,0:T(1,128)S(1)} %get-tuple-element.371) | copy-start | bytes 6148
  15.1 131.5 %copy-start.41 = (f32[1,512]{1,0:T(1,128)}, f32[1,512]{1,0:T(1,128)S(1)}, u32[]{:S(2)}) copy-start(f32[1,512]{1,0:T(1,128)S(1)} %get-tuple-element.372) | copy-start | bytes 6148
  15.1 131.5 %copy-start.43 = (f32[1,512]{1,0:T(1,128)}, f32[1,512]{1,0:T(1,128)S(1)}, u32[]{:S(2)}) copy-start(f32[1,512]{1,0:T(1,128)S(1)} %get-tuple-element.373) | copy-start | bytes 6148
  15.1 131.5 %copy-start.31 = (f32[2,4,512]{2,0,1:T(2,128)}, f32[2,4,512]{2,0,1:T(2,128)S(1)}, u32[]{:S(2)}) copy-start(f32[2,4,512]{2,0,1:T(2,128)S(1)} %convert_bitcast_fusion) | copy-start | bytes 49156
  37.1 101.2 %copy-start.46 = (bf16[2,512]{1,0:T(2,128)(2,1)}, bf16[2,512]{1,0:T(2,128)(2,1)S(1)}, u32[]{:S(2)}) copy-start(bf16[2,512]{1,0:T(2,128)(2,1)S(1)} %get-tuple-element.353) | copy-start | bytes 6148
  37.1 102.0 %copy-start.48 = (bf16[2,512]{1,0:T(2,128)(2,1)}, bf16[2,512]{1,0:T(2,128)(2,1)S(1)}, u32[]{:S(2)}) copy-start(bf16[2,512]{1,0:T(2,128)(2,1)S(1)} %get-tuple-element.354) | copy-start | bytes 6148
  37.1 102.8 %copy-start.50 = (bf16[2,512]{1,0:T(2,128)(2,1)}, bf16[2,512]{1,0:T(2,128)(2,1)S(1)}, u32[]{:S(2)}) copy-start(bf16[2,512]{1,0:T(2,128)(2,1)S(1)} %get-tuple-element.355) | copy-start | bytes 6148
  37.6 100.7 %copy-start.18 = (bf16[512,512]{1,0:T(8,128)(2,1)S(1)}, bf16[512,512]{1,0:T(8,128)(2,1)}, u32[]{:S(2)}) copy-start(bf16[512,512]{1,0:T(8,128)(2,1)} %param.23) | copy-start | bytes 1572868
  37.9 100.5 %copy-start.45 = (f32[512]{0:T(512)S(1)}, f32[512]{0:T(512)}, u32[]{:S(2)}) copy-start(f32[512]{0:T(512)} %param.24) | copy-start | bytes 6148
  754.5 70.9 %copy-start.57 = (f32[512]{0:T(512)S(1)}, f32[512]{0:T(512)}, u32[]{:S(2)}) copy-start(f32[512]{0:T(512)} %copy-done.56) | copy-start | bytes 6148
  825.5 29.2 %copy-start.62 = (f32[2,512]{1,0:T(2,128)S(1)}, f32[2,512]{1,0:T(2,128)}, u32[]{:S(2)}) copy-start(f32[2,512]{1,0:T(2,128)} %get-tuple-element.380) | copy-start | bytes 12292
  825.5 29.2 %copy-start.63 = (f32[2,512]{1,0:T(2,128)S(1)}, f32[2,512]{1,0:T(2,128)}, u32[]{:S(2)}) copy-start(f32[2,512]{1,0:T(2,128)} %get-tuple-element.381) | copy-start | bytes 12292
  825.5 29.2 %copy-start.64 = (f32[2,512]{1,0:T(2,128)S(1)}, f32[2,512]{1,0:T(2,128)}, u32[]{:S(2)}) copy-start(f32[2,512]{1,0:T(2,128)} %get-tuple-element.382) | copy-start | bytes 12292
  825.5 29.2 %copy-start.65 = (f32[2,512]{1,0:T(2,128)S(1)}, f32[2,512]{1,0:T(2,128)}, u32[]{:S(2)}) copy-start(f32[2,512]{1,0:T(2,128)} %get-tuple-element.383) | copy-start | bytes 12292
  825.5 29.2 %copy-start.66 = (f32[2,512]{1,0:T(2,128)S(1)}, f32[2,512]{1,0:T(2,128)}, u32[]{:S(2)}) copy-start(f32[2,512]{1,0:T(2,128)} %get-tuple-element.376) | copy-start | bytes 12292
  825.6 29.2 %copy-start.67 = (f32[2,512]{1,0:T(2,128)S(1)}, f32[2,512]{1,0:T(2,128)}, u32[]{:S(2)}) copy-start(f32[2,512]{1,0:T(2,128)} %get-tuple-element.377) | copy-start | bytes 12292
  825.6 29.2 %copy-start.80 = (s32[16]{0:T(128)S(1)}, s32[16]{0:T(128)}, u32[]{:S(2)}) copy-start(s32[16]{0:T(128)} %copy-done.79) | copy-start | bytes 196
  829.9 24.9 %copy-start.68 = (f32[2,512]{1,0:T(2,128)S(1)}, f32[2,512]{1,0:T(2,128)}, u32[]{:S(2)}) copy-start(f32[2,512]{1,0:T(2,128)} %get-tuple-element.378) | copy-start | bytes 12292
  830.0 24.9 %copy-start.69 = (f32[2,512]{1,0:T(2,128)S(1)}, f32[2,512]{1,0:T(2,128)}, u32[]{:S(2)}) copy-start(f32[2,512]{1,0:T(2,128)} %get-tuple-element.379) | copy-start | bytes 12292
  (137 other events, 380.2 us)
Sparse Core Ops, SparseCore 0:
  143.3 254.6 all-reduce.22
where the time goes:
time: 882 us; the launch traced here: 866 us
  local copies, waits for them, and re-layouts  275 us (31%)
  waiting for transfers between devices  250 us (28%)
  blocking collectives  214 us (24%)
  other arithmetic  89.9 us (10%)
  between operations  14.7 us (2%)
  matrix products  14 us (2%)
    psum x1, waiting for transfers between devices, local(): proj = lax.psum(partial_proj, 'tensor')  250 us
    pad x64, local copies, waits for them, and re-layouts, local_one_block(): cum_decay, cum_drive = lax.associative_scan(compose, (decay, drive), axis=0)  231 us
    psum x1, blocking collectives, local(): lax.psum(jnp.dot(dec_in, xproj_weight, preferred_element_type=jnp.float32...  100 us
    all_gather x2, blocking collectives, entering(): lax.all_gather(part.astype(kind), axis)  68.6 us
    add x32, other arithmetic, local_one_block(): cum_decay, cum_drive = lax.associative_scan(compose, (decay, drive), axis=0)  25.2 us
    mul x32, other arithmetic, compose(): return (earlier[0] * later[0], later[0] * earlier[1] + later[1])  24.1 us
    all_gather x1, blocking collectives, local(): states = lax.all_gather(final_state[None], 'group', axis=0, tiled=True)  23.7 us
    all_gather x1, blocking collectives, local(): tails = lax.all_gather(tail[None], 'group', axis=0, tiled=True)  21.7 us
  transfers between devices with their start and end apart: 2, of which 1 were waited for; matrix products, arithmetic and copies ran while one was open for 1% of the time, Pallas kernels for 0%

commit v1 on v0

v1 whole, which is shorter than its diff:
```python
import jax
import jax.numpy as jnp
from jax import lax
from jax.experimental import pallas as pl
from jax.experimental.pallas import tpu as pltpu
from jax.sharding import PartitionSpec as P

N = 16
R = 512
STEPS = 4
F32 = jnp.float32
BF16 = jnp.bfloat16
WIDE = 640
BLOCKS = 8


def silu(v):
    return v * jax.nn.sigmoid(v)


def softplus(v):
    return jnp.maximum(v, 0.0) + jnp.log1p(jnp.exp(-jnp.abs(v)))


def split_tail(total):
    rows = total.shape[0]
    low = total[:, :R].astype(BF16)
    tail = total[:, R:]
    head = tail.astype(BF16)
    rest = (tail - head.astype(F32)).astype(BF16)
    pad = jnp.zeros((rows, 128 - 4 * N), BF16)
    return low, jnp.concatenate([head, rest, pad], 1)


def conv_proj_kernel(x_ref, w_ref, b_ref, xw_ref, rate_ref, part_ref, cin_ref, nrate_ref, ext):
    rows, width = x_ref.shape
    ext[0:8, :] = jnp.zeros((8, width), F32)
    ext[8 : 8 + rows, :] = x_ref[...].astype(F32)
    w = w_ref[...].astype(F32)
    taps = w.shape[0]
    mixed = b_ref[...].astype(F32)
    for k in range(taps):
        mixed = mixed + w[k : k + 1] * ext[8 - (taps - 1) + k : 8 - (taps - 1) + k + rows, :]
    cin = silu(mixed).astype(BF16)
    cin_ref[...] = cin
    part = jnp.dot(cin, xw_ref[...], preferred_element_type=F32)
    part_ref[:, : R + 2 * N] = part.astype(BF16)
    part_ref[:, R + 2 * N :] = jnp.zeros((rows, WIDE - R - 2 * N), BF16)
    nrate_ref[...] = -jnp.transpose(rate_ref[...])


def middle_kernel(sp_ref, got_ref, tails_ref, x_ref, dx_ref, w_ref, b_ref, xw_ref, msg_ref, ein_ref):
    taps, width = w_ref.shape
    place = lax.axis_index("group")
    position = lax.rem(place, BLOCKS)
    w = w_ref[...].astype(F32)
    bias = b_ref[...].astype(F32)
    total = got_ref[0].astype(F32)
    for k in range(1, BLOCKS):
        total = total + got_ref[k].astype(F32)
    msg_ref[0:16, :] = total.astype(BF16)
    before = tails_ref[jnp.maximum(place - 1, 0)].astype(F32)
    before = jnp.where(position == 0, jnp.zeros_like(before), before)
    near = jnp.concatenate([before, x_ref[0:16, :].astype(F32)[0 : taps - 1]], 0)
    rim = bias
    for k in range(taps):
        rim = rim + w[k : k + 1] * near[k : k + taps - 1]
    first = tails_ref[BLOCKS - 1].astype(F32)
    second = tails_ref[2 * BLOCKS - 1].astype(F32)
    picked = [jnp.where(sp_ref[s] == 0, first, second) for s in range(2)]
    window = [
        jnp.concatenate([picked[0][k : k + 1], picked[1][k : k + 1]], 0) for k in range(taps - 1)
    ] + [dx_ref[t].astype(F32) for t in range(STEPS)]
    lines = []
    for t in range(STEPS):
        mixed = bias
        for k in range(taps):
            mixed = mixed + w[k : k + 1] * window[t + k]
        lines.append(mixed)
    extra = jnp.concatenate(lines + [rim, jnp.zeros((8 - (taps - 1), width), F32)], 0)
    ein = silu(extra).astype(BF16)
    ein_ref[...] = ein
    part = jnp.dot(ein, xw_ref[...], preferred_element_type=F32)
    msg_ref[16:32, : R + 2 * N] = part.astype(BF16)
    msg_ref[16:32, R + 2 * N :] = jnp.zeros((16, WIDE - R - 2 * N), BF16)


def sum_kernel(a_ref, b_ref, c_ref, d_ref, out_ref):
    width = R + 2 * N
    total = (a_ref[:, :width].astype(F32) + b_ref[:, :width].astype(F32)) + (
        c_ref[:, :width].astype(F32) + d_ref[:, :width].astype(F32)
    )
    low, tail = split_tail(total)
    for k in range(out_ref.shape[0]):
        out_ref[k, :, :R] = low
        out_ref[k, :, R:] = tail


def joined(block):
    return block + pltpu.roll(block, 128 - 2 * N, 1)


def scan_kernel(
    all_ref, cin_ref, ein_ref, dtw_ref, db_ref, nrate_ref,
    msg_ref, y_ref, reach_ref, bc_ref, dstep_ref, dbc_ref, u_ref, step_ref, low_ref,
):
    rows, width = cin_ref.shape
    ex = all_ref[0, 16:32, :].astype(F32)
    for k in range(1, BLOCKS):
        ex = ex + all_ref[k, 16:32, :].astype(F32)
    turned = jnp.concatenate([ex[8:16], ex[0:8]], 0)
    head = lax.broadcasted_iota(jnp.int32, (16, 1), 0) < 3
    for k in range(BLOCKS):
        low_ref[16 * k : 16 * k + 16, :] = all_ref[k, 0:16, :R]
        bc_ref[16 * k : 16 * k + 16, :] = joined(all_ref[k, 0:16, R:].astype(F32))
    low_ref[0:16, :] = jnp.where(head, turned[:, :R], all_ref[0, 0:16, :R].astype(F32)).astype(BF16)
    bc_ref[0:16, :] = jnp.where(head, joined(turned[:, R:]), bc_ref[0:16, :])
    low_ref[rows : rows + 16, :] = ex[:, :R].astype(BF16)
    step = softplus(
        jnp.dot(low_ref[...], dtw_ref[...], preferred_element_type=F32) + db_ref[...]
    )
    step_ref[...] = step[:rows]
    dstep_ref[...] = step[rows : rows + 8]
    dbc_ref[...] = jnp.transpose(
        jnp.concatenate([joined(ex[:, R:]), jnp.zeros((112, 128), F32)], 0)
    )[0 : 2 * N]
    u_ref[...] = step[:rows] * cin_ref[...].astype(F32)
    ein = ein_ref[...].astype(F32)
    u_ref[0:8, :] = jnp.where(head[0:8], step[0:8] * ein[8:16], u_ref[0:8, :])
    bct = jnp.transpose(bc_ref[...])[0 : 2 * N]
    nrate = nrate_ref[...]

    def group(g, carry):
        h, bc, total = carry
        at = pl.ds(pl.multiple_of(8 * g, 8), 8)
        d8 = step_ref[at, :]
        u8 = u_ref[at, :]
        values, sums = [], []
        for j in range(8):
            d = d8[j : j + 1]
            h = jnp.exp(nrate * d) * h + bc[0:N, j : j + 1] * u8[j : j + 1]
            values.append(jnp.sum(bc[N : 2 * N, j : j + 1] * h, axis=0, keepdims=True))
            total = total + d
            sums.append(total)
        y_ref[at, :] = jnp.concatenate(values, 0)
        reach_ref[at, :] = jnp.concatenate(sums, 0)
        return h, pltpu.roll(bc, 120, 1), total

    h, _, total = lax.fori_loop(
        0, rows // 8, group, (jnp.zeros((N, width), F32), bct, jnp.zeros((1, width), F32))
    )
    lanes = [total[:, 128 * k : 128 * k + 128] for k in range(width // 128)]
    coarse = jnp.concatenate(lanes, 0)
    fine = coarse - coarse.astype(BF16).astype(F32)
    side = jnp.concatenate([coarse, fine, jnp.zeros((8, 128), F32)], 0).astype(BF16)
    for k in range(msg_ref.shape[0]):
        msg_ref[k, :, :width] = h.astype(BF16)
        msg_ref[k, :, width:] = side


def finish_kernel(
    sp_ref, got_ref, y_ref, reach_ref, bc_ref, cin_ref, ein_ref, z_ref, dstep_ref, dbc_ref, dz_ref,
    skip_ref, nrate_ref, out_ref, dec_ref, in_ref,
):
    rows, width = y_ref.shape
    place = lax.axis_index("group")
    mine, position = lax.div(place, BLOCKS), lax.rem(place, BLOCKS)
    nrate = nrate_ref[...]
    skip = skip_ref[...]
    finals = []
    incoming = jnp.zeros((N, width), F32)
    for p in range(2):
        h = jnp.zeros((N, width), F32)
        for k in range(BLOCKS):
            r = p * BLOCKS + k
            if k > 0:
                incoming = jnp.where((mine == p) & (position == k), h, incoming)
            side = got_ref[r, :, width:].astype(F32)
            total = side[0:4] + side[4:8]
            total = jnp.concatenate([total[i : i + 1] for i in range(4)], 1)
            h = jnp.exp(nrate * total) * h + got_ref[r, :, :width].astype(F32)
        finals.append(h)
    in_ref[...] = incoming
    ein = ein_ref[...].astype(F32)

    def group(g, carry):
        at = pl.ds(pl.multiple_of(16 * g, 16), 16)
        s = reach_ref[at, :]
        c = bc_ref[at, :]
        acc = y_ref[at, :]
        for n in range(N):
            acc = acc + c[:, N + n : N + n + 1] * (
                in_ref[n : n + 1, :] * jnp.exp(nrate_ref[n : n + 1, :] * s)
            )
        cin = cin_ref[at, :].astype(F32)
        row = lax.broadcasted_iota(jnp.int32, (16, 1), 0) + 16 * g
        cin = jnp.where(row < 3, jnp.concatenate([ein[8:16], ein[0:8]], 0), cin)
        out_ref[at, :] = ((acc + skip * cin) * silu(z_ref[at, :].astype(F32))).astype(BF16)
        return carry

    lax.fori_loop(0, rows // 16, group, 0)
    states = [jnp.where(sp_ref[s] == 0, finals[0], finals[1]) for s in range(2)]
    for t in range(STEPS):
        values = []
        for s in range(2):
            r = 2 * t + s
            d = dstep_ref[r : r + 1, :]
            u = ein[r : r + 1]
            states[s] = jnp.exp(nrate * d) * states[s] + dbc_ref[0:N, r : r + 1] * (d * u)
            values.append(
                jnp.sum(dbc_ref[N : 2 * N, r : r + 1] * states[s], axis=0, keepdims=True) + skip * u
            )
        value = jnp.concatenate(values, 0) * silu(dz_ref[t].astype(F32))
        dec_ref[t] = value.astype(BF16)


def call(kernel, outs, scratch=(), smem=0, inputs=1, name=None):
    vmem = pl.BlockSpec(memory_space=pltpu.VMEM)
    return pl.pallas_call(
        kernel,
        out_shape=outs,
        in_specs=[pl.BlockSpec(memory_space=pltpu.SMEM)] * smem + [vmem] * inputs,
        out_specs=jax.tree.map(lambda _: vmem, outs),
        scratch_shapes=list(scratch),
        compiler_params=pltpu.CompilerParams(vmem_limit_bytes=48 * 1024 * 1024),
        name=name,
    )


def shape(*dims, kind=F32):
    return jax.ShapeDtypeStruct(dims, kind)


def local(
    x_prompt,
    z_prompt,
    conv_weight,
    conv_bias,
    xproj_weight,
    dtproj_weight,
    dt_bias,
    decay_rate,
    skip_gain,
    sample_prompt,
    decode_x,
    decode_z,
):
    rows, width = x_prompt.shape
    taps = conv_weight.shape[0]
    places = lax.axis_size("group")
    ring = lax.axis_size("tensor")
    bias = conv_bias.reshape(1, width)
    dbias = dt_bias.reshape(1, width)
    skip = skip_gain.reshape(1, width)

    tail = x_prompt[rows - (taps - 1) :]
    tails = lax.all_to_all(
        jnp.broadcast_to(tail[None], (places, taps - 1, width)), "group", 0, 0
    )
    part, cin, nrate = call(
        conv_proj_kernel,
        (shape(rows, WIDE, kind=BF16), shape(rows, width, kind=BF16), shape(N, width)),
        [pltpu.VMEM((rows + 8, width), F32)],
        inputs=5,
        name="conv_proj",
    )(x_prompt, conv_weight, bias, xproj_weight, decay_rate)

    near = [[BLOCKS * a + j for j in range(BLOCKS)] for a in range(ring // BLOCKS)]
    got = lax.all_to_all(
        part.reshape(BLOCKS, rows // BLOCKS, WIDE), "tensor", 0, 0, axis_index_groups=near
    )
    msg, ein = call(
        middle_kernel,
        (shape(32, WIDE, kind=BF16), shape(16, width, kind=BF16)),
        smem=1,
        inputs=7,
        name="middle",
    )(sample_prompt, got, tails, x_prompt, decode_x, conv_weight, bias, xproj_weight)

    others = [
        lax.ppermute(msg, "tensor", [(i, (i + hop) % ring) for i in range(ring)])
        for hop in (2 * BLOCKS, BLOCKS, 3 * BLOCKS)
    ]
    spread = call(
        sum_kernel, shape(BLOCKS, 32, WIDE, kind=BF16), inputs=4, name="sums"
    )(msg, *others)
    everything = lax.all_to_all(spread, "tensor", 0, 0, axis_index_groups=near)

    send, y, reach, bc, dstep, dbc = call(
        scan_kernel,
        (
            shape(places, N, width + 128, kind=BF16),
            shape(rows, width),
            shape(rows, width),
            shape(rows, 128),
            shape(8, width),
            shape(2 * N, 128),
        ),
        [
            pltpu.VMEM((rows, width), F32),
            pltpu.VMEM((rows, width), F32),
            pltpu.VMEM((rows + 16, R), BF16),
        ],
        inputs=6,
        name="scan",
    )(everything, cin, ein, dtproj_weight, dbias, nrate)
    states = lax.all_to_all(send, "group", 0, 0)

    return call(
        finish_kernel,
        (shape(rows, width, kind=BF16), shape(STEPS, 2, width, kind=BF16)),
        [pltpu.VMEM((N, width), F32)],
        smem=1,
        inputs=12,
        name="finish",
    )(sample_prompt, states, y, reach, bc, cin, ein, z_prompt, dstep, dbc, decode_z, skip, nrate)


def solution(mesh):
    placed = (
        P("group", "tensor"),
        P("group", "tensor"),
        P(None, "tensor"),
        P("tensor"),
        P("tensor", None),
        P(None, "tensor"),
        P("tensor"),
        P("tensor", None),
        P("tensor"),
        P("group"),
        P(None, "group", "tensor"),
        P(None, "group", "tensor"),
    )
    return jax.shard_map(
        local,
        mesh=mesh,
        in_specs=placed,
        out_specs=(P("group", "tensor"), P(None, "group", "tensor")),
        check_vma=False,
    )
```

time: 882 us -> 91.4 us (0.10); the launches traced: 866 us -> 90.8 us
  local copies, waits for them, and re-layouts: 275 us -> 4.28 us
  waiting for transfers between devices: 250 us -> 8.58 us
  blocking collectives: 214 us -> 38.4 us
  other arithmetic: 89.9 us -> 0 us
  starting transfers between devices: 6.37 us -> 32.4 us
  matrix products: 14 us -> 0 us
  between operations: 14.7 us -> 0.77 us
    psum x1 -> x0, waiting for transfers between devices: 250 us -> none  [local(): proj = lax.psum(partial_proj, 'tensor')]
    pad x64 -> x0, local copies, waits for them, and re-layouts: 231 us -> none  [local_one_block(): cum_decay, cum_drive = lax.associative_scan(compose, (decay, drive), axis=0)]
    all_gather x4 -> x0, blocking collectives: 114 us -> none  [the longest x2 68.6 us: entering(): lax.all_gather(part.astype(kind), axis)]
    psum x1 -> x0, blocking collectives: 100 us -> none  [local(): lax.psum(jnp.dot(dec_in, xproj_weight, preferred_element_type=jnp.float32...]
    all_to_all x0 -> x3, blocking collectives: none -> 38.4 us  [the longest x1 16.5 us: local(): states = lax.all_to_all(send, 'group', 0, 0)]
    add x42 -> x0, other arithmetic: 34.7 us -> none  [the longest x32 25.2 us: local_one_block(): cum_decay, cum_drive = lax.associative_scan(compose, (decay, drive), axis=0)]
    mul x40 -> x0, other arithmetic: 28.1 us -> none  [the longest x32 24.1 us: compose(): return (earlier[0] * later[0], later[0] * earlier[1] + later[1])]
    while x208 -> x0, local copies, waits for them, and re-layouts: 17.4 us -> none
  transfers between devices with their start and end apart: 2 -> 4, of which waited for: 1 -> 2; matrix products, arithmetic and copies ran while one was open for 1% -> 2% of each run, Pallas kernels for 0% -> 0%
where the time goes in v1:
time: 91.4 us; the launch traced here: 90.8 us
  blocking collectives  38.4 us (42%)
  starting transfers between devices  32.4 us (35%)
  waiting for transfers between devices  8.58 us (9%)
  Pallas kernels  6.43 us (7%)
  local copies, waits for them, and re-layouts  4.28 us (5%)
    ppermute x3, starting transfers between devices, local(): lax.ppermute(msg, 'tensor', [(i, (i + hop) % ring) for i in range(ring)])  22.1 us
    all_to_all x1, blocking collectives, local(): states = lax.all_to_all(send, 'group', 0, 0)  16.5 us
    all_to_all x1, blocking collectives, local(): everything = lax.all_to_all(spread, 'tensor', 0, 0, axis_index_groups=near)  11.6 us
    all_to_all x1, blocking collectives, local(): lax.all_to_all(part.reshape(BLOCKS, rows // BLOCKS, WIDE), 'tensor', 0, 0...  10.3 us
    all_to_all x1, starting transfers between devices, local(): lax.all_to_all(jnp.broadcast_to(tail[None], (places, taps - 1, width)), '...  10.3 us
    all_to_all x1, waiting for transfers between devices, local(): lax.all_to_all(jnp.broadcast_to(tail[None], (places, taps - 1, width)), '...  5.4 us
    ppermute x3, waiting for transfers between devices, local(): lax.ppermute(msg, 'tensor', [(i, (i + hop) % ring) for i in range(ring)])  3.18 us
    unnamed x24, local copies, waits for them, and re-layouts  2.92 us
  transfers between devices with their start and end apart: 4, of which 2 were waited for; matrix products, arithmetic and copies ran while one was open for 2% of the time, Pallas kernels for 0%

profile of v1, /device:TPU:1, one launch (start us, length us, event | category | flops | bytes accessed | tf_op | source)
XLA Modules:
  0.0 90.8 jit_solution(6315682690237858050)
XLA Ops:
  0.6 0.7 slice.3
  1.3 0.7 broadcast_in_dim.2
  2.0 10.3 %all-to-all-start.1 = ((bf16[16,3,512]{2,1,0:T(4,128)(2,1)}), bf16[16,3,512]{2,1,0:T(4,128)(2,1)S(1)}, u32[]{:S(2)}, u32[]{:S(2)}) async-start(bf16[16,3,512]{2,1,0:T(4,128)(2,1)} %broadcast_in_dim.2), calls=%async_computation.1 | async-start | bytes 131072 | tf_op jit(solution)/shard_map/all_to_all | solution.py:257
  12.3 0.1 copy.15.rate_ref
  12.4 0.0 copy-start
  12.5 0.0 copy-start.3
  12.5 1.4 %copy.14.xw_ref = bf16[512,544]{1,0:T(8,128)(2,1)S(1)} copy(bf16[512,544]{0,1:T(8,128)(2,1)} %param.16) | data formatting | bytes 1114112 | tf_op args[4]
  13.9 0.4 conv_proj.1
  14.3 5.4 %all-to-all-done.1.tails_ref = bf16[16,3,512]{2,1,0:T(4,128)(2,1)S(1)} async-done(((bf16[16,3,512]{2,1,0:T(4,128)(2,1)}), bf16[16,3,512]{2,1,0:T(4,128)(2,1)S(1)}, u32[]{:S(2)}, u32[]{:S(2)}) %all-to-all-start.1) | async-done | bytes 49184 | tf_op jit(solution)/shard_map/all_to_all | solution.py:257
  19.7 10.3 %all_to_all.20.got_ref = bf16[8,16,640]{2,1,0:T(8,128)(2,1)S(1)} all-to-all(bf16[8,16,640]{2,1,0:T(8,128)(2,1)S(1)} %bitcast.3), channel_id=1, replica_groups={{0,1,2,3,4,5,6,7},{8,9,10,11,12,13,14,15},{16,17,18,19,20,21,22,23},{24..., dimensions={0} | all-to-all | bytes 327680 | tf_op jit(solution)/shard_map/all_to_all | solution.py:269
  30.0 0.8 middle.1
  30.8 9.9 %collective-permute-start.2 = (bf16[32,640]{1,0:T(8,128)(2,1)S(1)}, bf16[32,640]{1,0:T(8,128)(2,1)S(1)}, u32[]{:S(2)}, u32[]{:S(2)}) collective-permute-start(bf16[32,640]{1,0:T(8,128)(2,1)S(1)} %get-tuple-element.14.a_ref), channel_id=1, source_target_pairs={{0,24},{1,25},{2,26},{3,27},{4,28},{5,29},{6,30},{7,31},{8,0},{9,1... | collective-permute-start | bytes 122888 | tf_op jit(solution)/shard_map/ppermute | solution.py:281
  40.7 1.9 %collective-permute-start.1 = (bf16[32,640]{1,0:T(8,128)(2,1)S(1)}, bf16[32,640]{1,0:T(8,128)(2,1)S(1)}, u32[]{:S(2)}, u32[]{:S(2)}) collective-permute-start(bf16[32,640]{1,0:T(8,128)(2,1)S(1)} %get-tuple-element.14.a_ref), channel_id=1, source_target_pairs={{0,8},{1,9},{2,10},{3,11},{4,12},{5,13},{6,14},{7,15},{8,16},{9,17... | collective-permute-start | bytes 122888 | tf_op jit(solution)/shard_map/ppermute | solution.py:281
  42.6 10.3 %collective-permute-start = (bf16[32,640]{1,0:T(8,128)(2,1)S(1)}, bf16[32,640]{1,0:T(8,128)(2,1)S(1)}, u32[]{:S(2)}, u32[]{:S(2)}) collective-permute-start(bf16[32,640]{1,0:T(8,128)(2,1)S(1)} %get-tuple-element.14.a_ref), channel_id=1, source_target_pairs={{0,16},{1,17},{2,18},{3,19},{4,20},{5,21},{6,22},{7,23},{8,24},{9,... | collective-permute-start | bytes 122888 | tf_op jit(solution)/shard_map/ppermute | solution.py:281
  52.9 0.0 collective-permute-done.1.c_ref
  52.9 3.2 %collective-permute-done.b_ref = bf16[32,640]{1,0:T(8,128)(2,1)S(1)} collective-permute-done((bf16[32,640]{1,0:T(8,128)(2,1)S(1)}, bf16[32,640]{1,0:T(8,128)(2,1)S(1)}, u32[]{:S(2)}, u32[]{:S(2)}) %collective-permute-start) | collective-permute-done | bytes 40992 | tf_op jit(solution)/shard_map/ppermute | solution.py:281
  56.1 0.1 sums.1
  56.2 11.6 %all_to_all.21.all_ref = bf16[8,32,640]{2,1,0:T(8,128)(2,1)S(1)} all-to-all(bf16[8,32,640]{2,1,0:T(8,128)(2,1)S(1)} %sums.1), channel_id=1, replica_groups={{0,1,2,3,4,5,6,7},{8,9,10,11,12,13,14,15},{16,17,18,19,20,21,22,23},{24..., dimensions={0} | all-to-all | bytes 655360 | tf_op jit(solution)/shard_map/all_to_all | solution.py:287
  67.8 0.7 copy-done.7
  68.4 2.7 %scan.1 = (bf16[16,16,640]{2,1,0:T(8,128)(2,1)S(1)}, f32[128,512]{1,0:T(8,128)S(1)}, f32[128,512]{1,0:T(8,128)S(1)}, f32[128,128]{1,0:T(8,128)S(1)}, f32[8,512]{1,0:T(8,128)S(1)}, /*index=5*/f32[32,128]{1,0:T(8,128)S(1)}) custom-call(bf16[8,32,640]{2,1,0:T(8,128)(2,1)S(1)} %all_to_all.21.all_ref, bf16[128,512]{1,0:T(8,128)(2,1)S(1)} %get-tuple-element.15.cin_ref, ...), custom_call_target="tpu_custom_call" | custom-call | tf_op jit(solution)/shard_map/scan/pallas_call | solution.py:289
  71.1 0.0 copy-start.2
  71.1 16.5 %all_to_all.22.got_ref = bf16[16,16,640]{2,1,0:T(8,128)(2,1)S(1)} all-to-all(bf16[16,16,640]{2,1,0:T(8,128)(2,1)S(1)} %get-tuple-element.18), channel_id=1, replica_groups=mesh['group'=16,'tensor'=32] {'group'}, dimensions={0} | all-to-all | bytes 655360 | tf_op jit(solution)/shard_map/all_to_all | solution.py:307
  87.6 0.7 copy-done.5
  88.3 2.5 %finish.1 = (bf16[128,512]{1,0:T(8,128)(2,1)}, bf16[4,2,512]{2,1,0:T(2,128)(2,1)}) custom-call(s32[2]{0:T(128)S(1)} %copy-done.6, bf16[16,16,640]{2,1,0:T(8,128)(2,1)S(1)} %all_to_all.22.got_ref, f32[128,512]{1,0:T(8,128)S(1)} %get-tuple-element.19.y_ref, f32[128,512]{1,0:T(8,128)S(1)} %get-tuple-element.20.reach_ref, ...), custom_call_target="tpu_custom_call" | custom-call | tf_op jit(solution)/shard_map/finish/pallas_call | solution.py:309
  (19 shorter events, 0.0 us)
Async XLA Ops:
  2.0 10.3 %copy-start.10 = (bf16[512]{0:T(512)(128)(2,1)S(1)}, bf16[512]{0:T(512)(128)(2,1)}, u32[]{:S(2)}) copy-start(bf16[512]{0:T(512)(128)(2,1)} %param.15) | copy-start | bytes 3076
  2.0 10.3 %copy-start.9 = (f32[512,16]{0,1:T(8,128)S(1)}, f32[512,16]{0,1:T(8,128)}, u32[]{:S(2)}) copy-start(f32[512,16]{0,1:T(8,128)} %param.19) | copy-start | bytes 98308
  2.0 17.7 %all-to-all-start.1 = ((bf16[16,3,512]{2,1,0:T(4,128)(2,1)}), bf16[16,3,512]{2,1,0:T(4,128)(2,1)S(1)}, u32[]{:S(2)}, u32[]{:S(2)}) async-start(bf16[16,3,512]{2,1,0:T(4,128)(2,1)} %broadcast_in_dim.2), calls=%async_computation.1 | async-start | bytes 131072 | tf_op jit(solution)/shard_map/all_to_all | solution.py:257
  12.4 1.4 %copy-start = (bf16[128,512]{1,0:T(8,128)(2,1)S(1)}, bf16[128,512]{1,0:T(8,128)(2,1)}, u32[]{:S(2)}) copy-start(bf16[128,512]{1,0:T(8,128)(2,1)} %x_ref.3) | copy-start | bytes 393220
  12.5 1.4 %copy-start.3 = (bf16[4,512]{1,0:T(4,128)(2,1)S(1)}, bf16[4,512]{1,0:T(4,128)(2,1)}, u32[]{:S(2)}) copy-start(bf16[4,512]{1,0:T(4,128)(2,1)} %w_ref.3) | copy-start | bytes 12292
  19.7 10.3 %copy-start.4 = (bf16[4,2,512]{2,1,0:T(2,128)(2,1)S(1)}, bf16[4,2,512]{2,1,0:T(2,128)(2,1)}, u32[]{:S(2)}) copy-start(bf16[4,2,512]{2,1,0:T(2,128)(2,1)} %dx_ref.1) | copy-start | bytes 24580
  19.7 10.3 %copy-start.6 = (s32[2]{0:T(128)S(1)}, s32[2]{0:T(128)}, u32[]{:S(2)}) copy-start(s32[2]{0:T(128)} %sp_ref.3) | copy-start | bytes 28
  30.8 37.0 %copy-start.1 = (bf16[512,512]{1,0:T(8,128)(2,1)S(1)}, bf16[512,512]{1,0:T(8,128)(2,1)}, u32[]{:S(2)}) copy-start(bf16[512,512]{1,0:T(8,128)(2,1)} %dtw_ref.1) | copy-start | bytes 1572868
  30.8 22.1 %collective-permute-start.2 = (bf16[32,640]{1,0:T(8,128)(2,1)S(1)}, bf16[32,640]{1,0:T(8,128)(2,1)S(1)}, u32[]{:S(2)}, u32[]{:S(2)}) collective-permute-start(bf16[32,640]{1,0:T(8,128)(2,1)S(1)} %get-tuple-element.14.a_ref), channel_id=1, source_target_pairs={{0,24},{1,25},{2,26},{3,27},{4,28},{5,29},{6,30},{7,31},{8,0},{9,1... | collective-permute-start | bytes 122888 | tf_op jit(solution)/shard_map/ppermute | solution.py:281
  40.7 12.2 %collective-permute-start.1 = (bf16[32,640]{1,0:T(8,128)(2,1)S(1)}, bf16[32,640]{1,0:T(8,128)(2,1)S(1)}, u32[]{:S(2)}, u32[]{:S(2)}) collective-permute-start(bf16[32,640]{1,0:T(8,128)(2,1)S(1)} %get-tuple-element.14.a_ref), channel_id=1, source_target_pairs={{0,8},{1,9},{2,10},{3,11},{4,12},{5,13},{6,14},{7,15},{8,16},{9,17... | collective-permute-start | bytes 122888 | tf_op jit(solution)/shard_map/ppermute | solution.py:281
  42.6 13.5 %collective-permute-start = (bf16[32,640]{1,0:T(8,128)(2,1)S(1)}, bf16[32,640]{1,0:T(8,128)(2,1)S(1)}, u32[]{:S(2)}, u32[]{:S(2)}) collective-permute-start(bf16[32,640]{1,0:T(8,128)(2,1)S(1)} %get-tuple-element.14.a_ref), channel_id=1, source_target_pairs={{0,16},{1,17},{2,18},{3,19},{4,20},{5,21},{6,22},{7,23},{8,24},{9,... | collective-permute-start | bytes 122888 | tf_op jit(solution)/shard_map/ppermute | solution.py:281
  67.8 0.7 copy-start.7
  71.1 16.5 %copy-start.2 = (bf16[128,512]{1,0:T(8,128)(2,1)S(1)}, bf16[128,512]{1,0:T(8,128)(2,1)}, u32[]{:S(2)}) copy-start(bf16[128,512]{1,0:T(8,128)(2,1)} %z_ref.1) | copy-start | bytes 393220
  87.6 0.7 copy-start.5
  87.6 0.7 copy-start.8

commit v2 on v1

v2 whole, which is shorter than its diff:
```python
import jax
import jax.numpy as jnp
from jax import lax
from jax.experimental import pallas as pl
from jax.experimental.pallas import tpu as pltpu
from jax.sharding import PartitionSpec as P

N = 16
R = 512
STEPS = 4
F32 = jnp.float32
BF16 = jnp.bfloat16
WIDE = 640
BLOCKS = 8
NEAR = 8


def silu(v):
    return v * jax.nn.sigmoid(v)


def softplus(v):
    return jnp.maximum(v, 0.0) + jnp.log1p(jnp.exp(-jnp.abs(v)))


def folded(tile, line):
    lane = lax.broadcasted_iota(jnp.int32, tile.shape, 1)
    four = jnp.concatenate([line[:, 128 * i : 128 * i + 128] for i in range(4)], 0)
    last = pltpu.roll(line[:, R:], 64, 1)
    side = jnp.concatenate([pltpu.roll(four, 64, 1), four, last, jnp.zeros((7, 128), F32)], 0)
    return jnp.where(lane < 64, tile, side)


def unfolded(tile):
    lane = lax.broadcasted_iota(jnp.int32, (4, 128), 1)
    four = jnp.where(lane < 64, pltpu.roll(tile[0:4], 64, 1), tile[4:8])
    return jnp.concatenate([four[i : i + 1] for i in range(4)], 1), pltpu.roll(tile[8:9], 64, 1)


def with_rest(tile):
    lane = lax.broadcasted_iota(jnp.int32, tile.shape, 1)
    row = lax.broadcasted_iota(jnp.int32, tile.shape, 0)
    head = tile.astype(BF16).astype(F32)
    rest = pltpu.roll(tile - head, 2 * N, 1)
    plain = (lax.rem(lane, 64) < 2 * N) | ((lane >= 64) & (row < 8))
    return jnp.where(plain, head, rest)


def joined(block):
    return block + pltpu.roll(block, 128 - 2 * N, 1)


def onto(rows, columns_ref):
    return lax.dot_general(
        rows, columns_ref[...], (((1,), (1,)), ((), ())), preferred_element_type=F32
    )


def edge_kernel(x_ref, out_ref):
    rows = x_ref.shape[0]
    tail = x_ref[rows - 16 :, :].astype(F32)[8:].astype(BF16)
    for k in range(out_ref.shape[0]):
        out_ref[k] = tail


def prepare_kernel(
    sp_ref, x_ref, w_ref, b_ref, rate_ref, z_ref, dz_ref, db_ref, skip_ref,
    cin_ref, nrate_ref, gate_ref, small_ref, ext,
):
    rows, width = x_ref.shape
    ext[0:8, :] = jnp.zeros((8, width), F32)
    ext[8 : 8 + rows, :] = x_ref[...].astype(F32)
    w = w_ref[...].astype(F32)
    taps = w.shape[0]
    bias = b_ref[...].astype(F32).reshape(1, width)
    mixed = bias
    for k in range(taps):
        mixed = mixed + w[k : k + 1] * ext[9 - taps + k : 9 - taps + k + rows, :]
    cin_ref[...] = silu(mixed).astype(BF16)
    nrate_ref[...] = -rate_ref[...]
    gate_ref[...] = silu(z_ref[...].astype(F32))
    small_ref[0:8, :] = jnp.concatenate(
        [
            db_ref[...].reshape(1, width),
            skip_ref[...].reshape(1, width),
            bias,
            jnp.zeros((1, width), F32),
            w,
        ],
        0,
    )
    for s in range(2):
        small_ref[16 + s : 17 + s, :] = jnp.full((1, width), sp_ref[s], jnp.int32).astype(F32)
    small_ref[8:16, :] = silu(jnp.concatenate([dz_ref[t].astype(F32) for t in range(STEPS)], 0))


def project_kernel(
    tails_ref, cin_ref, x_ref, dx_ref, small_ref, xw_ref, part_ref, all_ref
):
    rows, width = cin_ref.shape
    taps = STEPS
    place = lax.axis_index("group")
    position = lax.rem(place, BLOCKS)
    bias = small_ref[2:3, :]
    w = small_ref[4 : 4 + taps, :]
    before = tails_ref[jnp.maximum(place - 1, 0)].astype(F32)[9 - taps :]
    before = jnp.where(position == 0, jnp.zeros_like(before), before)
    near = jnp.concatenate([before, x_ref[0:16, :].astype(F32)[0 : taps - 1]], 0)
    rim = bias
    for k in range(taps):
        rim = rim + w[k : k + 1] * near[k : k + taps - 1]
    first = tails_ref[BLOCKS - 1].astype(F32)[9 - taps :]
    second = tails_ref[2 * BLOCKS - 1].astype(F32)[9 - taps :]
    picked = [jnp.where(small_ref[16 + s : 17 + s, :] < 0.5, first, second) for s in range(2)]
    window = [
        jnp.concatenate([picked[0][k : k + 1], picked[1][k : k + 1]], 0) for k in range(taps - 1)
    ] + [dx_ref[t].astype(F32) for t in range(STEPS)]
    lines = []
    for t in range(STEPS):
        mixed = bias
        for k in range(taps):
            mixed = mixed + w[k : k + 1] * window[t + k]
        lines.append(mixed)
    extra = silu(jnp.concatenate([rim, jnp.zeros((8 - (taps - 1), width), F32)] + lines, 0))
    row = lax.broadcasted_iota(jnp.int32, (16, 1), 0)
    start = jnp.where(row < taps - 1, extra, cin_ref[0:16, :].astype(F32))
    all_ref[0:16, :] = start.astype(BF16)
    all_ref[16:rows, :] = cin_ref[16:rows, :]
    all_ref[rows : rows + 16, :] = jnp.concatenate(
        [extra[8:16], jnp.zeros((8, width), F32)], 0
    ).astype(BF16)
    part = onto(all_ref[...], xw_ref)
    full = jnp.concatenate([part, jnp.zeros((rows + 16, WIDE - R - 2 * N), F32)], 1)
    for k in range(part_ref.shape[0]):
        mine = full[16 * k : 16 * k + 16]
        part_ref[k, :, :R] = mine[:, :R].astype(BF16)
        part_ref[k, :, R:] = folded(mine[:, R:], full[rows + k : rows + k + 1]).astype(BF16)


def near_sum_kernel(got_ref, out_ref):
    total = got_ref[0].astype(F32)
    for k in range(1, got_ref.shape[0]):
        total = total + got_ref[k].astype(F32)
    total = total.astype(BF16)
    for k in range(out_ref.shape[0]):
        out_ref[k] = total


def far_sum_kernel(got_ref, out_ref):
    total = (got_ref[0].astype(F32) + got_ref[1].astype(F32)) + (
        got_ref[2].astype(F32) + got_ref[3].astype(F32)
    )
    low = total[:, :R].astype(BF16)
    tile = with_rest(total[:, R:]).astype(BF16)
    for k in range(out_ref.shape[0]):
        out_ref[k, :, :R] = low
        out_ref[k, :, R:] = tile


def parts(value):
    head = value.astype(BF16)
    return head, (value - head.astype(F32)).astype(BF16)


def step_kernel(
    all_ref, cin_ref, dtw_ref, small_ref, nrate_ref,
    msg_ref, step_ref, bc_ref, u_ref, dbc_ref, low_ref, left_ref,
):
    rows, width = u_ref.shape
    lines, tiles = [], []
    for k in range(NEAR):
        at = slice(16 * k, 16 * k + 16)
        tile = all_ref[k, :, R:].astype(F32)
        low_ref[at, :] = all_ref[k, :, :R]
        bc_ref[at, :] = joined(tile)
        line, tile = unfolded(tile)
        lines.append(line)
        tiles.append(tile)
    low_ref[rows : rows + 16, :] = jnp.concatenate(
        lines + [jnp.zeros((8, width), F32)], 0
    ).astype(BF16)
    dbc_ref[...] = joined(jnp.concatenate(tiles, 0))
    step = softplus(
        jnp.dot(low_ref[...], dtw_ref[...], preferred_element_type=F32) + small_ref[0:1, :]
    )
    step_ref[...] = step
    step = step[:rows]
    u_ref[...] = step * cin_ref[0:rows, :].astype(F32)
    down = lax.broadcasted_iota(jnp.int32, (rows, rows), 0)
    over = lax.broadcasted_iota(jnp.int32, (rows, rows), 1)
    after = jnp.where(over > down, 1.0, 0.0).astype(BF16)
    left = sum(jnp.dot(after, part, preferred_element_type=F32) for part in parts(step))
    left_ref[...] = left
    ends = []
    for n in range(N):
        rate = nrate_ref[n : n + 1, :]
        acc = jnp.zeros((16, width), F32)
        for g in range(rows // 16):
            at = slice(16 * g, 16 * g + 16)
            acc = acc + jnp.exp(rate * left_ref[at, :]) * (bc_ref[at, n : n + 1] * u_ref[at, :])
        ends.append(jnp.sum(acc, axis=0, keepdims=True))
    total = left[0:1] + step[0:1]
    coarse = jnp.concatenate([total[:, 128 * k : 128 * k + 128] for k in range(width // 128)], 0)
    fine = coarse - coarse.astype(BF16).astype(F32)
    side = jnp.concatenate([coarse, fine, jnp.zeros((8, 128), F32)], 0)
    result = jnp.concatenate([jnp.concatenate(ends, 0), side], 1).astype(BF16)
    for k in range(msg_ref.shape[0]):
        msg_ref[k] = result


def scan_kernel(
    step_ref, u_ref, bc_ref, cin_ref, gate_ref, small_ref, nrate_ref, dbc_ref,
    out_ref, reach_ref, from_ref, dout_ref,
):
    rows, width = u_ref.shape
    down = lax.broadcasted_iota(jnp.int32, (rows, rows), 0)
    over = lax.broadcasted_iota(jnp.int32, (rows, rows), 1)
    upto = jnp.where(over <= down, 1.0, 0.0).astype(BF16)
    reach_ref[...] = sum(
        jnp.dot(upto, part, preferred_element_type=F32) for part in parts(step_ref[0:rows, :])
    )
    dbc = jnp.transpose(jnp.concatenate([dbc_ref[...], jnp.zeros((120, 128), F32)], 0))
    nrate = nrate_ref[...]
    skip = small_ref[1:2, :]
    bct = jnp.transpose(bc_ref[...])[0 : 2 * N]

    def group(g, carry):
        h, bc = carry
        at = pl.ds(pl.multiple_of(8 * g, 8), 8)
        d8 = step_ref[at, :]
        u8 = u_ref[at, :]
        values = []
        for j in range(8):
            h = jnp.exp(nrate * d8[j : j + 1]) * h + bc[0:N, j : j + 1] * u8[j : j + 1]
            values.append(jnp.sum(bc[N : 2 * N, j : j + 1] * h, axis=0, keepdims=True))
        out_ref[at, :] = jnp.concatenate(values, 0)
        return h, pltpu.roll(bc, 120, 1)

    lax.fori_loop(0, rows // 8, group, (jnp.zeros((N, width), F32), bct))
    out_ref[...] = (out_ref[...] + skip * cin_ref[0:rows, :].astype(F32)) * gate_ref[...]
    dec = cin_ref[rows : rows + 16, :].astype(F32)
    own = []
    kept = [jnp.ones((N, width), F32) for _ in range(2)]
    state = [jnp.zeros((N, width), F32) for _ in range(2)]
    for r in range(2 * STEPS):
        s = r % 2
        d = step_ref[rows + r : rows + r + 1, :]
        decay = jnp.exp(nrate * d)
        kept[s] = decay * kept[s]
        state[s] = decay * state[s] + dbc[0:N, r : r + 1] * (d * dec[r : r + 1])
        c = dbc[N : 2 * N, r : r + 1]
        from_ref[r] = c * kept[s]
        own.append(jnp.sum(c * state[s], axis=0, keepdims=True))
    dout_ref[...] = jnp.concatenate(own, 0) + skip * dec[0 : 2 * STEPS]


def finish_kernel(
    sp_ref, got_ref, y_ref, reach_ref, bc_ref, gate_ref, nrate_ref, small_ref, from_ref, own_ref,
    out_ref, dec_ref, in_ref,
):
    rows, width = y_ref.shape
    place = lax.axis_index("group")
    mine, position = lax.div(place, BLOCKS), lax.rem(place, BLOCKS)
    nrate = nrate_ref[...]
    finals = []
    incoming = jnp.zeros((N, width), F32)
    for p in range(2):
        h = jnp.zeros((N, width), F32)
        for k in range(BLOCKS):
            r = p * BLOCKS + k
            if k > 0:
                incoming = jnp.where((mine == p) & (position == k), h, incoming)
            side = got_ref[r, :, width:].astype(F32)
            total = side[0:4] + side[4:8]
            total = jnp.concatenate([total[i : i + 1] for i in range(4)], 1)
            h = jnp.exp(nrate * total) * h + got_ref[r, :, :width].astype(F32)
        finals.append(h)
    in_ref[...] = incoming

    def group(g, carry):
        at = pl.ds(pl.multiple_of(16 * g, 16), 16)
        s = reach_ref[at, :]
        c = bc_ref[at, :]
        acc = jnp.zeros((16, width), F32)
        for n in range(N):
            acc = acc + c[:, N + n : N + n + 1] * (
                in_ref[n : n + 1, :] * jnp.exp(nrate_ref[n : n + 1, :] * s)
            )
        out_ref[at, :] = (y_ref[at, :] + acc * gate_ref[at, :]).astype(BF16)
        return carry

    lax.fori_loop(0, rows // 16, group, 0)
    states = [jnp.where(sp_ref[s] == 0, finals[0], finals[1]) for s in range(2)]
    for t in range(STEPS):
        pair = [
            jnp.sum(from_ref[2 * t + s] * states[s], axis=0, keepdims=True) for s in range(2)
        ]
        at = slice(2 * t, 2 * t + 2)
        value = (jnp.concatenate(pair, 0) + own_ref[at, :]) * small_ref[8 + 2 * t : 10 + 2 * t, :]
        dec_ref[t] = value.astype(BF16)


def call(kernel, outs, scratch=(), smem=0, hbm=0, inputs=0, name=None):
    vmem = pl.BlockSpec(memory_space=pltpu.VMEM)
    return pl.pallas_call(
        kernel,
        out_shape=outs,
        in_specs=[pl.BlockSpec(memory_space=pltpu.SMEM)] * smem
        + [pl.BlockSpec(memory_space=pl.ANY)] * hbm
        + [vmem] * inputs,
        out_specs=jax.tree.map(lambda _: vmem, outs),
        scratch_shapes=list(scratch),
        compiler_params=pltpu.CompilerParams(vmem_limit_bytes=24 * 1024 * 1024),
        name=name,
    )


def shape(*dims, kind=F32):
    return jax.ShapeDtypeStruct(dims, kind)


def local(
    x_prompt,
    z_prompt,
    conv_weight,
    conv_bias,
    xproj_weight,
    dtproj_weight,
    dt_bias,
    decay_rate,
    skip_gain,
    sample_prompt,
    decode_x,
    decode_z,
):
    rows, width = x_prompt.shape
    taps = conv_weight.shape[0]
    places = lax.axis_size("group")
    ring = lax.axis_size("tensor")
    deep = NEAR // 2
    near = [
        [NEAR * a + 2 * ((j + a) % deep) + y for j in range(deep) for y in range(2)]
        for a in range(ring // NEAR)
    ]
    far = [[g[j] for g in near] for j in range(NEAR)]

    tail = call(
        edge_kernel, shape(places, 8, width, kind=BF16), inputs=1, name="edge"
    )(x_prompt)
    tails = lax.all_to_all(tail, "group", 0, 0)
    cin, nrate, gate, small = call(
        prepare_kernel,
        (shape(rows, width, kind=BF16), shape(N, width), shape(rows, width), shape(24, width)),
        [pltpu.VMEM((rows + 8, width), F32)],
        smem=1,
        inputs=8,
        name="prepare",
    )(
        sample_prompt,
        x_prompt,
        conv_weight,
        conv_bias,
        decay_rate.T,
        z_prompt,
        decode_z,
        dt_bias,
        skip_gain,
    )
    part, cin = call(
        project_kernel,
        (shape(NEAR, 16, WIDE, kind=BF16), shape(rows + 16, width, kind=BF16)),
        inputs=6,
        name="project",
    )(tails, cin, x_prompt, decode_x, small, xproj_weight.T)

    got = lax.all_to_all(part, "tensor", 0, 0, axis_index_groups=near)
    sums = call(
        near_sum_kernel, shape(ring // NEAR, 16, WIDE, kind=BF16), inputs=1, name="near_sum"
    )(got)
    got = lax.all_to_all(sums, "tensor", 0, 0, axis_index_groups=far)
    sums = call(far_sum_kernel, shape(NEAR, 16, WIDE, kind=BF16), inputs=1, name="far_sum")(got)
    everything = lax.all_to_all(sums, "tensor", 0, 0, axis_index_groups=near)

    send, step, bc, u, dbc = call(
        step_kernel,
        (
            shape(places, N, width + 128, kind=BF16),
            shape(rows + 16, width),
            shape(rows, 128),
            shape(rows, width),
            shape(8, 128),
        ),
        [pltpu.VMEM((rows + 16, R), BF16), pltpu.VMEM((rows, width), F32)],
        inputs=5,
        name="step",
    )(everything, cin, dtproj_weight, small, nrate)
    states = lax.all_to_all(send, "group", 0, 0)
    y, reach, share, own = call(
        scan_kernel,
        (
            shape(rows, width),
            shape(rows, width),
            shape(2 * STEPS, N, width),
            shape(2 * STEPS, width),
        ),
        inputs=8,
        name="scan",
    )(step, u, bc, cin, gate, small, nrate, dbc)
    return call(
        finish_kernel,
        (shape(rows, width, kind=BF16), shape(STEPS, 2, width, kind=BF16)),
        [pltpu.VMEM((N, width), F32)],
        smem=1,
        inputs=9,
        name="finish",
    )(sample_prompt, states, y, reach, bc, gate, nrate, small, share, own)


def solution(mesh):
    placed = (
        P("group", "tensor"),
        P("group", "tensor"),
        P(None, "tensor"),
        P("tensor"),
        P("tensor", None),
        P(None, "tensor"),
        P("tensor"),
        P("tensor", None),
        P("tensor"),
        P("group"),
        P(None, "group", "tensor"),
        P(None, "group", "tensor"),
    )
    return jax.shard_map(
        local,
        mesh=mesh,
        in_specs=placed,
        out_specs=(P("group", "tensor"), P(None, "group", "tensor")),
        check_vma=False,
    )
```

time: 91.4 us -> 84.4 us (0.923)
  starting transfers between devices: 32.4 us -> 18.3 us
  waiting for transfers between devices: 8.58 us -> 13.1 us
  Pallas kernels: 6.43 us -> 9.36 us
  local copies, waits for them, and re-layouts: 4.28 us -> 2.6 us
  blocking collectives: 38.4 us -> 39.9 us
    ppermute x3 -> x0, starting transfers between devices: 22.1 us -> none  [local(): lax.ppermute(msg, 'tensor', [(i, (i + hop) % ring) for i in range(ring)])]
    all_to_all x1 -> x2, starting transfers between devices: 10.3 us -> 18.3 us  [the longest x1 10.3 us: local(): tails = lax.all_to_all(tail, 'group', 0, 0)]
    all_to_all x1 -> x2, waiting for transfers between devices: 5.4 us -> 13.1 us  [the longest x1 6.91 us: local(): states = lax.all_to_all(send, 'group', 0, 0)]
    ppermute x3 -> x0, waiting for transfers between devices: 3.18 us -> none  [local(): lax.ppermute(msg, 'tensor', [(i, (i + hop) % ring) for i in range(ring)])]
    pallas_call x4 -> x7, Pallas kernels: 3.96 us -> 7.03 us  [the longest x1 2.66 us: local(): call(scan_kernel, (shape(rows, width), shape(rows, width), shape(2 * STEP...]
    all_to_all x3, blocking collectives: 38.4 us -> 39.9 us  [the longest x1 19.3 us: local(): got = lax.all_to_all(sums, 'tensor', 0, 0, axis_index_groups=far)]
    unnamed x24 -> x26, local copies, waits for them, and re-layouts: 2.92 us -> 2.6 us
  transfers between devices with their start and end apart: 4 -> 2, of which waited for: 2 -> 2; matrix products, arithmetic and copies ran while one was open for 2% -> 0% of each run, Pallas kernels for 0% -> 4%
where the time goes in v2:
time: 84.4 us; the launch traced here: 84 us
  blocking collectives  39.9 us (47%)
  starting transfers between devices  18.3 us (22%)
  waiting for transfers between devices  13.1 us (16%)
  Pallas kernels  9.36 us (11%)
  local copies, waits for them, and re-layouts  2.6 us (3%)
    all_to_all x1, blocking collectives, local(): got = lax.all_to_all(sums, 'tensor', 0, 0, axis_index_groups=far)  19.3 us
    all_to_all x1, blocking collectives, local(): everything = lax.all_to_all(sums, 'tensor', 0, 0, axis_index_groups=near)  10.4 us
    all_to_all x1, starting transfers between devices, local(): tails = lax.all_to_all(tail, 'group', 0, 0)  10.3 us
    all_to_all x1, blocking collectives, local(): got = lax.all_to_all(part, 'tensor', 0, 0, axis_index_groups=near)  10.2 us
    all_to_all x1, starting transfers between devices, local(): states = lax.all_to_all(send, 'group', 0, 0)  7.97 us
    all_to_all x1, waiting for transfers between devices, local(): states = lax.all_to_all(send, 'group', 0, 0)  6.91 us
    all_to_all x1, waiting for transfers between devices, local(): tails = lax.all_to_all(tail, 'group', 0, 0)  6.16 us
    pallas_call x1, Pallas kernels, local(): call(scan_kernel, (shape(rows, width), shape(rows, width), shape(2 * STEP...  2.66 us
  transfers between devices with their start and end apart: 2, of which 2 were waited for; matrix products, arithmetic and copies ran while one was open for 0% of the time, Pallas kernels for 4%

profile of v2, /device:TPU:1, one launch (start us, length us, event | category | flops | bytes accessed | tf_op | source)
XLA Modules:
  0.0 84.0 jit_solution(7541549837598595768)
XLA Ops:
  0.6 0.0 copy-start
  0.6 0.9 %copy-done = bf16[128,512]{1,0:T(8,128)(2,1)S(1)} copy-done((bf16[128,512]{1,0:T(8,128)(2,1)S(1)}, bf16[128,512]{1,0:T(8,128)(2,1)}, u32[]{:S(2)}) %copy-start) | copy-done | bytes 131096
  1.6 0.0 copy-start.10
  1.6 0.7 edge.1
  2.2 10.3 %all-to-all-start = ((bf16[16,8,512]{2,1,0:T(8,128)(2,1)}), bf16[16,8,512]{2,1,0:T(8,128)(2,1)S(1)}, u32[]{:S(2)}, u32[]{:S(2)}) async-start(bf16[16,8,512]{2,1,0:T(8,128)(2,1)} %edge.1), calls=%async_computation | async-start | bytes 262144 | tf_op jit(solution)/shard_map/all_to_all | solution.py:350
  12.5 0.0 copy-start.12
  12.6 0.0 copy-done.5
  12.6 0.0 copy-done.7
  12.6 0.0 copy-done.8
  12.6 0.6 copy-done.11
  13.2 0.0 copy-done.12
  13.2 0.9 %prepare.1 = (bf16[128,512]{1,0:T(8,128)(2,1)S(1)}, f32[16,512]{1,0:T(8,128)S(1)}, f32[128,512]{1,0:T(8,128)S(1)}, f32[24,512]{1,0:T(8,128)S(1)}) custom-call(s32[2]{0:T(128)S(1)} %copy-done.11, bf16[128,512]{1,0:T(8,128)(2,1)S(1)} %copy-done.1, bf16[4,512]{1,0:T(4,128)(2,1)S(1)} %copy-done.8, bf16[512]{0:T(512)(128)(2,1)S(1)} %copy-done.12, ...), custom_call_target="tpu_custom_call" | custom-call | tf_op jit(solution)/shard_map/prepare/pallas_call | solution.py:351
  14.1 6.2 %all-to-all-done.tails_ref = bf16[16,8,512]{2,1,0:T(8,128)(2,1)S(1)} async-done(((bf16[16,8,512]{2,1,0:T(8,128)(2,1)}), bf16[16,8,512]{2,1,0:T(8,128)(2,1)S(1)}, u32[]{:S(2)}, u32[]{:S(2)}) %all-to-all-start) | async-done | bytes 131104 | tf_op jit(solution)/shard_map/all_to_all | solution.py:350
  20.3 1.1 %copy-done.2 = bf16[512,544]{0,1:T(8,128)(2,1)S(1)} copy-done((bf16[512,544]{0,1:T(8,128)(2,1)S(1)}, bf16[512,544]{0,1:T(8,128)(2,1)}, u32[]{:S(2)}) %copy-start.2) | copy-done | bytes 557080
  21.3 0.4 project.1
  21.8 10.2 %all_to_all.25.got_ref = bf16[8,16,640]{2,1,0:T(8,128)(2,1)S(1)} all-to-all(bf16[8,16,640]{2,1,0:T(8,128)(2,1)S(1)} %get-tuple-element.19), channel_id=1, replica_groups={{0,1,2,3,4,5,6,7},{10,11,12,13,14,15,8,9},{20,21,22,23,16,17,18,19},{30..., dimensions={0} | all-to-all | bytes 327680 | tf_op jit(solution)/shard_map/all_to_all | solution.py:376
  32.0 19.3 %all_to_all.26.got_ref = bf16[4,16,640]{2,1,0:T(8,128)(2,1)S(1)} all-to-all(bf16[4,16,640]{2,1,0:T(8,128)(2,1)S(1)} %near_sum.1), channel_id=1, replica_groups={{0,10,20,30},{1,11,21,31},{2,12,22,24},{3,13,23,25},{4,14,16,26},{5,15,..., dimensions={0} | all-to-all | bytes 163840 | tf_op jit(solution)/shard_map/all_to_all | solution.py:380
  51.3 0.1 far_sum.1
  51.4 10.4 %all_to_all.27.all_ref = bf16[8,16,640]{2,1,0:T(8,128)(2,1)S(1)} all-to-all(bf16[8,16,640]{2,1,0:T(8,128)(2,1)S(1)} %far_sum.1), channel_id=1, replica_groups={{0,1,2,3,4,5,6,7},{10,11,12,13,14,15,8,9},{20,21,22,23,16,17,18,19},{30..., dimensions={0} | all-to-all | bytes 327680 | tf_op jit(solution)/shard_map/all_to_all | solution.py:382
  61.8 2.3 %step.1 = (bf16[16,16,640]{2,1,0:T(8,128)(2,1)}, f32[144,512]{1,0:T(8,128)S(1)}, f32[128,128]{1,0:T(8,128)S(1)}, f32[128,512]{1,0:T(8,128)S(1)}, f32[8,128]{1,0:T(8,128)S(1)}) custom-call(bf16[8,16,640]{2,1,0:T(8,128)(2,1)S(1)} %all_to_all.27.all_ref, bf16[144,512]{1,0:T(8,128)(2,1)S(1)} %get-tuple-element.20.cin_ref, bf16[512,512]{1,0:T(8,128)(2,1)S(1)} %copy-done.3, ...), custom_call_target="tpu_custom_call" | custom-call | tf_op jit(solution)/shard_map/step/pallas_call | solution.py:384
  64.1 8.0 %all-to-all-start.4 = ((bf16[16,16,640]{2,1,0:T(8,128)(2,1)}), bf16[16,16,640]{2,1,0:T(8,128)(2,1)S(1)}, u32[]{:S(2)}, u32[]{:S(2)}) async-start(bf16[16,16,640]{2,1,0:T(8,128)(2,1)} %get-tuple-element.22), calls=%async_computation.4 | async-start | bytes 655360 | tf_op jit(solution)/shard_map/all_to_all | solution.py:397
  72.1 2.7 %scan.1 = (f32[128,512]{1,0:T(8,128)S(1)}, f32[128,512]{1,0:T(8,128)S(1)}, f32[8,16,512]{2,1,0:T(8,128)S(1)}, f32[8,512]{1,0:T(8,128)S(1)}) custom-call(f32[144,512]{1,0:T(8,128)S(1)} %get-tuple-element.23.step_ref, f32[128,512]{1,0:T(8,128)S(1)} %get-tuple-element.24.u_ref, f32[128,128]{1,0:T(8,128)S(1)} %get-tuple-element.25.bc_ref, ...), custom_call_target="tpu_custom_call" | custom-call | tf_op jit(solution)/shard_map/scan/pallas_call | solution.py:398
  74.7 6.9 %all-to-all-done.4.got_ref = bf16[16,16,640]{2,1,0:T(8,128)(2,1)S(1)} async-done(((bf16[16,16,640]{2,1,0:T(8,128)(2,1)}), bf16[16,16,640]{2,1,0:T(8,128)(2,1)S(1)}, u32[]{:S(2)}, u32[]{:S(2)}) %all-to-all-start.4) | async-done | bytes 327712 | tf_op jit(solution)/shard_map/all_to_all | solution.py:397
  81.6 2.3 %finish.1 = (bf16[128,512]{1,0:T(8,128)(2,1)}, bf16[4,2,512]{2,1,0:T(2,128)(2,1)}) custom-call(s32[2]{0:T(128)S(1)} %copy-done.11, bf16[16,16,640]{2,1,0:T(8,128)(2,1)S(1)} %all-to-all-done.4.got_ref, f32[128,512]{1,0:T(8,128)S(1)} %get-tuple-element.28.y_ref, f32[128,512]{1,0:T(8,128)S(1)} %get-tuple-element.29.reach_ref, ...), custom_call_target="tpu_custom_call" | custom-call | tf_op jit(solution)/shard_map/finish/pallas_call | solution.py:409
  (17 shorter events, 0.1 us)
Async XLA Ops:
  0.6 0.9 %copy-start = (bf16[128,512]{1,0:T(8,128)(2,1)S(1)}, bf16[128,512]{1,0:T(8,128)(2,1)}, u32[]{:S(2)}) copy-start(bf16[128,512]{1,0:T(8,128)(2,1)} %x_ref.5) | copy-start | bytes 393220
  1.5 11.0 %copy-start.5 = (f32[512,16]{0,1:T(8,128)S(1)}, f32[512,16]{0,1:T(8,128)}, u32[]{:S(2)}) copy-start(f32[512,16]{0,1:T(8,128)} %param.19) | copy-start | bytes 98308
  1.5 11.0 %copy-start.7 = (bf16[4,2,512]{2,1,0:T(2,128)(2,1)S(1)}, bf16[4,2,512]{2,1,0:T(2,128)(2,1)}, u32[]{:S(2)}) copy-start(bf16[4,2,512]{2,1,0:T(2,128)(2,1)} %dz_ref.1) | copy-start | bytes 24580
  1.5 11.0 %copy-start.8 = (bf16[4,512]{1,0:T(4,128)(2,1)S(1)}, bf16[4,512]{1,0:T(4,128)(2,1)}, u32[]{:S(2)}) copy-start(bf16[4,512]{1,0:T(4,128)(2,1)} %w_ref.1) | copy-start | bytes 12292
  1.5 11.0 %copy-start.9 = (f32[512]{0:T(512)S(1)}, f32[512]{0:T(512)}, u32[]{:S(2)}) copy-start(f32[512]{0:T(512)} %db_ref.1) | copy-start | bytes 6148
  1.6 11.1 %copy-start.10 = (f32[512]{0:T(512)S(1)}, f32[512]{0:T(512)}, u32[]{:S(2)}) copy-start(f32[512]{0:T(512)} %skip_ref.1) | copy-start | bytes 6148
  2.2 10.4 %copy-start.1 = (bf16[128,512]{1,0:T(8,128)(2,1)S(1)}, bf16[128,512]{1,0:T(8,128)(2,1)}, u32[]{:S(2)}) copy-start(bf16[128,512]{1,0:T(8,128)(2,1)} %x_ref.5) | copy-start | bytes 393220
  2.2 10.4 %copy-start.4 = (bf16[128,512]{1,0:T(8,128)(2,1)S(1)}, bf16[128,512]{1,0:T(8,128)(2,1)}, u32[]{:S(2)}) copy-start(bf16[128,512]{1,0:T(8,128)(2,1)} %z_ref.1) | copy-start | bytes 393220
  2.2 18.0 %all-to-all-start = ((bf16[16,8,512]{2,1,0:T(8,128)(2,1)}), bf16[16,8,512]{2,1,0:T(8,128)(2,1)S(1)}, u32[]{:S(2)}, u32[]{:S(2)}) async-start(bf16[16,8,512]{2,1,0:T(8,128)(2,1)} %edge.1), calls=%async_computation | async-start | bytes 262144 | tf_op jit(solution)/shard_map/all_to_all | solution.py:350
  12.5 0.7 copy-start.11
  12.5 0.7 copy-start.12
  13.2 7.0 %copy-start.6 = (bf16[4,2,512]{2,1,0:T(2,128)(2,1)S(1)}, bf16[4,2,512]{2,1,0:T(2,128)(2,1)}, u32[]{:S(2)}) copy-start(bf16[4,2,512]{2,1,0:T(2,128)(2,1)} %dx_ref.1) | copy-start | bytes 24580
  20.3 1.1 %copy-start.2 = (bf16[512,544]{0,1:T(8,128)(2,1)S(1)}, bf16[512,544]{0,1:T(8,128)(2,1)}, u32[]{:S(2)}) copy-start(bf16[512,544]{0,1:T(8,128)(2,1)} %param.16) | copy-start | bytes 1671172
  31.9 29.9 %copy-start.3 = (bf16[512,512]{1,0:T(8,128)(2,1)S(1)}, bf16[512,512]{1,0:T(8,128)(2,1)}, u32[]{:S(2)}) copy-start(bf16[512,512]{1,0:T(8,128)(2,1)} %dtw_ref.1) | copy-start | bytes 1572868
  64.1 17.5 %all-to-all-start.4 = ((bf16[16,16,640]{2,1,0:T(8,128)(2,1)}), bf16[16,16,640]{2,1,0:T(8,128)(2,1)S(1)}, u32[]{:S(2)}, u32[]{:S(2)}) async-start(bf16[16,16,640]{2,1,0:T(8,128)(2,1)} %get-tuple-element.22), calls=%async_computation.4 | async-start | bytes 655360 | tf_op jit(solution)/shard_map/all_to_all | solution.py:397

commit v3 on v2

--- a/solution.py
+++ b/solution.py
@@ -56,16 +56,9 @@
     )
 
 
-def edge_kernel(x_ref, out_ref):
-    rows = x_ref.shape[0]
-    tail = x_ref[rows - 16 :, :].astype(F32)[8:].astype(BF16)
-    for k in range(out_ref.shape[0]):
-        out_ref[k] = tail
-
-
 def prepare_kernel(
-    sp_ref, x_ref, w_ref, b_ref, rate_ref, z_ref, dz_ref, db_ref, skip_ref,
-    cin_ref, nrate_ref, gate_ref, small_ref, ext,
+    sp_ref, x_ref, w_ref, b_ref, xw_ref, rate_ref, z_ref, dz_ref, db_ref, skip_ref,
+    part_ref, cin_ref, nrate_ref, gate_ref, small_ref, ext,
 ):
     rows, width = x_ref.shape
     ext[0:8, :] = jnp.zeros((8, width), F32)
@@ -76,7 +69,10 @@
     mixed = bias
     for k in range(taps):
         mixed = mixed + w[k : k + 1] * ext[9 - taps + k : 9 - taps + k + rows, :]
-    cin_ref[...] = silu(mixed).astype(BF16)
+    cin = silu(mixed).astype(BF16)
+    cin_ref[...] = cin
+    part_ref[:, : R + 2 * N] = onto(cin, xw_ref)
+    part_ref[:, R + 2 * N :] = jnp.zeros((rows, WIDE - R - 2 * N), F32)
     nrate_ref[...] = -rate_ref[...]
     gate_ref[...] = silu(z_ref[...].astype(F32))
     small_ref[0:8, :] = jnp.concatenate(
@@ -95,22 +91,22 @@
 
 
 def project_kernel(
-    tails_ref, cin_ref, x_ref, dx_ref, small_ref, xw_ref, part_ref, all_ref
+    tails_ref, main_ref, cin_ref, x_ref, dx_ref, small_ref, xw_ref, part_ref, all_ref
 ):
     rows, width = cin_ref.shape
-    taps = STEPS
+    taps = tails_ref.shape[1] + 1
     place = lax.axis_index("group")
     position = lax.rem(place, BLOCKS)
     bias = small_ref[2:3, :]
     w = small_ref[4 : 4 + taps, :]
-    before = tails_ref[jnp.maximum(place - 1, 0)].astype(F32)[9 - taps :]
+    before = tails_ref[jnp.maximum(place - 1, 0)].astype(F32)
     before = jnp.where(position == 0, jnp.zeros_like(before), before)
     near = jnp.concatenate([before, x_ref[0:16, :].astype(F32)[0 : taps - 1]], 0)
     rim = bias
     for k in range(taps):
         rim = rim + w[k : k + 1] * near[k : k + taps - 1]
-    first = tails_ref[BLOCKS - 1].astype(F32)[9 - taps :]
-    second = tails_ref[2 * BLOCKS - 1].astype(F32)[9 - taps :]
+    first = tails_ref[BLOCKS - 1].astype(F32)
+    second = tails_ref[2 * BLOCKS - 1].astype(F32)
     picked = [jnp.where(small_ref[16 + s : 17 + s, :] < 0.5, first, second) for s in range(2)]
     window = [
         jnp.concatenate([picked[0][k : k + 1], picked[1][k : k + 1]], 0) for k in range(taps - 1)
@@ -129,12 +125,14 @@
     all_ref[rows : rows + 16, :] = jnp.concatenate(
         [extra[8:16], jnp.zeros((8, width), F32)], 0
     ).astype(BF16)
-    part = onto(all_ref[...], xw_ref)
-    full = jnp.concatenate([part, jnp.zeros((rows + 16, WIDE - R - 2 * N), F32)], 1)
+    extra = onto(extra.astype(BF16), xw_ref)
+    extra = jnp.concatenate([extra, jnp.zeros((16, WIDE - R - 2 * N), F32)], 1)
     for k in range(part_ref.shape[0]):
-        mine = full[16 * k : 16 * k + 16]
+        mine = main_ref[16 * k : 16 * k + 16, :]
+        if k == 0:
+            mine = jnp.where(row < taps - 1, extra, mine)
         part_ref[k, :, :R] = mine[:, :R].astype(BF16)
-        part_ref[k, :, R:] = folded(mine[:, R:], full[rows + k : rows + k + 1]).astype(BF16)
+        part_ref[k, :, R:] = folded(mine[:, R:], extra[8 + k : 9 + k]).astype(BF16)
 
 
 def near_sum_kernel(got_ref, out_ref):
@@ -255,7 +253,7 @@
 
 
 def finish_kernel(
-    sp_ref, got_ref, y_ref, reach_ref, bc_ref, gate_ref, nrate_ref, small_ref, from_ref, own_ref,
+    got_ref, y_ref, reach_ref, bc_ref, gate_ref, nrate_ref, small_ref, from_ref, own_ref,
     out_ref, dec_ref, in_ref,
 ):
     rows, width = y_ref.shape
@@ -290,7 +288,9 @@
         return carry
 
     lax.fori_loop(0, rows // 16, group, 0)
-    states = [jnp.where(sp_ref[s] == 0, finals[0], finals[1]) for s in range(2)]
+    states = [
+        jnp.where(small_ref[16 + s : 17 + s, :] < 0.5, finals[0], finals[1]) for s in range(2)
+    ]
     for t in range(STEPS):
         pair = [
             jnp.sum(from_ref[2 * t + s] * states[s], axis=0, keepdims=True) for s in range(2)
@@ -344,22 +344,30 @@
     ]
     far = [[g[j] for g in near] for j in range(NEAR)]
 
-    tail = call(
-        edge_kernel, shape(places, 8, width, kind=BF16), inputs=1, name="edge"
-    )(x_prompt)
-    tails = lax.all_to_all(tail, "group", 0, 0)
-    cin, nrate, gate, small = call(
+    tail = x_prompt[rows - (taps - 1) :]
+    tails = lax.all_to_all(
+        jnp.broadcast_to(tail[None], (places, taps - 1, width)), "group", 0, 0
+    )
+    columns = xproj_weight.T
+    main, cin, nrate, gate, small = call(
         prepare_kernel,
-        (shape(rows, width, kind=BF16), shape(N, width), shape(rows, width), shape(24, width)),
+        (
+            shape(rows, WIDE),
+            shape(rows, width, kind=BF16),
+            shape(N, width),
+            shape(rows, width),
+            shape(24, width),
+        ),
         [pltpu.VMEM((rows + 8, width), F32)],
         smem=1,
-        inputs=8,
+        inputs=9,
         name="prepare",
     )(
         sample_prompt,
         x_prompt,
         conv_weight,
         conv_bias,
+        columns,
         decay_rate.T,
         z_prompt,
         decode_z,
@@ -369,9 +377,9 @@
     part, cin = call(
         project_kernel,
         (shape(NEAR, 16, WIDE, kind=BF16), shape(rows + 16, width, kind=BF16)),
-        inputs=6,
+        inputs=7,
         name="project",
-    )(tails, cin, x_prompt, decode_x, small, xproj_weight.T)
+    )(tails, main, cin, x_prompt, decode_x, small, columns)
 
     got = lax.all_to_all(part, "tensor", 0, 0, axis_index_groups=near)
     sums = call(
@@ -410,10 +418,9 @@
         finish_kernel,
         (shape(rows, width, kind=BF16), shape(STEPS, 2, width, kind=BF16)),
         [pltpu.VMEM((N, width), F32)],
-        smem=1,
         inputs=9,
         name="finish",
-    )(sample_prompt, states, y, reach, bc, gate, nrate, small, share, own)
+    )(states, y, reach, bc, gate, nrate, small, share, own)
 
 
 def solution(mesh):

time: 84.4 us -> 82.8 us (0.981)
  waiting for transfers between devices: 13.1 us -> 10.6 us
  local copies, waits for them, and re-layouts: 2.6 us -> 4.03 us
  Pallas kernels: 9.36 us -> 8.18 us
    all_to_all x1, waiting for transfers between devices: 6.16 us -> 3.77 us  [local(): lax.all_to_all(jnp.broadcast_to(tail[None], (places, taps - 1, width)), '...]
where the time goes in v3:
time: 82.8 us; the launch traced here: 82.2 us
  blocking collectives  39.9 us (48%)
  starting transfers between devices  18.7 us (23%)
  waiting for transfers between devices  10.6 us (13%)
  Pallas kernels  8.18 us (10%)
  local copies, waits for them, and re-layouts  4.03 us (5%)
    all_to_all x1, blocking collectives, local(): got = lax.all_to_all(sums, 'tensor', 0, 0, axis_index_groups=far)  19.3 us
    all_to_all x1, blocking collectives, local(): everything = lax.all_to_all(sums, 'tensor', 0, 0, axis_index_groups=near)  10.4 us
    all_to_all x1, starting transfers between devices, local(): lax.all_to_all(jnp.broadcast_to(tail[None], (places, taps - 1, width)), '...  10.3 us
    all_to_all x1, blocking collectives, local(): got = lax.all_to_all(part, 'tensor', 0, 0, axis_index_groups=near)  10.2 us
    all_to_all x1, starting transfers between devices, local(): states = lax.all_to_all(send, 'group', 0, 0)  8.41 us
    all_to_all x1, waiting for transfers between devices, local(): states = lax.all_to_all(send, 'group', 0, 0)  6.85 us
    all_to_all x1, waiting for transfers between devices, local(): lax.all_to_all(jnp.broadcast_to(tail[None], (places, taps - 1, width)), '...  3.77 us
    pallas_call x1, Pallas kernels, local(): call(scan_kernel, (shape(rows, width), shape(rows, width), shape(2 * STEP...  2.66 us
  transfers between devices with their start and end apart: 2, of which 2 were waited for; matrix products, arithmetic and copies ran while one was open for 0% of the time, Pallas kernels for 4%

profile of v3, /device:TPU:1, one launch (start us, length us, event | category | flops | bytes accessed | tf_op | source)
XLA Modules:
  0.0 82.2 jit_solution(835558780399022348)
XLA Ops:
  0.6 0.0 copy-start.2
  0.6 0.8 slice.3
  1.4 0.7 broadcast_in_dim.2
  2.1 10.3 %all-to-all-start = ((bf16[16,3,512]{2,1,0:T(4,128)(2,1)}), bf16[16,3,512]{2,1,0:T(4,128)(2,1)S(1)}, u32[]{:S(2)}, u32[]{:S(2)}) async-start(bf16[16,3,512]{2,1,0:T(4,128)(2,1)} %broadcast_in_dim.2), calls=%async_computation | async-start | bytes 131072 | tf_op jit(solution)/shard_map/all_to_all | solution.py:348
  12.4 0.0 copy-start.11
  12.4 0.0 copy-start.12
  12.5 0.6 copy-done.9
  13.1 0.0 copy-done.11
  13.1 1.1 %copy-done = bf16[512,544]{0,1:T(8,128)(2,1)S(1)} copy-done((bf16[512,544]{0,1:T(8,128)(2,1)S(1)}, bf16[512,544]{0,1:T(8,128)(2,1)}, u32[]{:S(2)}) %copy-start) | copy-done | bytes 557080
  14.1 0.9 %copy-done.4 = bf16[128,512]{1,0:T(8,128)(2,1)S(1)} copy-done((bf16[128,512]{1,0:T(8,128)(2,1)S(1)}, bf16[128,512]{1,0:T(8,128)(2,1)}, u32[]{:S(2)}) %copy-start.4) | copy-done | bytes 131096
  15.0 1.0 %prepare.1 = (f32[128,640]{1,0:T(8,128)S(1)}, bf16[128,512]{1,0:T(8,128)(2,1)S(1)}, f32[16,512]{1,0:T(8,128)S(1)}, f32[128,512]{1,0:T(8,128)S(1)}, f32[24,512]{1,0:T(8,128)S(1)}) custom-call(s32[2]{0:T(128)S(1)} %copy-done.12, bf16[128,512]{1,0:T(8,128)(2,1)S(1)} %copy-done.2, bf16[4,512]{1,0:T(4,128)(2,1)S(1)} %copy-done.8, bf16[512]{0:T(512)(128)(2,1)S(1)} %copy-done.11, ...), custom_call_target="tpu_custom_call" | custom-call | tf_op jit(solution)/shard_map/prepare/pallas_call | solution.py:352
  16.0 3.8 %all-to-all-done.tails_ref = bf16[16,3,512]{2,1,0:T(4,128)(2,1)S(1)} async-done(((bf16[16,3,512]{2,1,0:T(4,128)(2,1)}), bf16[16,3,512]{2,1,0:T(4,128)(2,1)S(1)}, u32[]{:S(2)}, u32[]{:S(2)}) %all-to-all-start) | async-done | bytes 49184 | tf_op jit(solution)/shard_map/all_to_all | solution.py:348
  19.8 0.0 copy-done.7
  19.8 0.3 project.1
  20.2 10.2 %all_to_all.25.got_ref = bf16[8,16,640]{2,1,0:T(8,128)(2,1)S(1)} all-to-all(bf16[8,16,640]{2,1,0:T(8,128)(2,1)S(1)} %get-tuple-element.21), channel_id=1, replica_groups={{0,1,2,3,4,5,6,7},{10,11,12,13,14,15,8,9},{20,21,22,23,16,17,18,19},{30..., dimensions={0} | all-to-all | bytes 327680 | tf_op jit(solution)/shard_map/all_to_all | solution.py:384
  30.4 19.3 %all_to_all.26.got_ref = bf16[4,16,640]{2,1,0:T(8,128)(2,1)S(1)} all-to-all(bf16[4,16,640]{2,1,0:T(8,128)(2,1)S(1)} %near_sum.1), channel_id=1, replica_groups={{0,10,20,30},{1,11,21,31},{2,12,22,24},{3,13,23,25},{4,14,16,26},{5,15,..., dimensions={0} | all-to-all | bytes 163840 | tf_op jit(solution)/shard_map/all_to_all | solution.py:388
  49.7 0.1 far_sum.1
  49.8 10.4 %all_to_all.27.all_ref = bf16[8,16,640]{2,1,0:T(8,128)(2,1)S(1)} all-to-all(bf16[8,16,640]{2,1,0:T(8,128)(2,1)S(1)} %far_sum.1), channel_id=1, replica_groups={{0,1,2,3,4,5,6,7},{10,11,12,13,14,15,8,9},{20,21,22,23,16,17,18,19},{30..., dimensions={0} | all-to-all | bytes 327680 | tf_op jit(solution)/shard_map/all_to_all | solution.py:390
  60.2 0.0 copy-done.3
  60.2 2.3 %step.1 = (bf16[16,16,640]{2,1,0:T(8,128)(2,1)}, f32[144,512]{1,0:T(8,128)S(1)}, f32[128,128]{1,0:T(8,128)S(1)}, f32[128,512]{1,0:T(8,128)S(1)}, f32[8,128]{1,0:T(8,128)S(1)}) custom-call(bf16[8,16,640]{2,1,0:T(8,128)(2,1)S(1)} %all_to_all.27.all_ref, bf16[144,512]{1,0:T(8,128)(2,1)S(1)} %get-tuple-element.22.cin_ref, bf16[512,512]{1,0:T(8,128)(2,1)S(1)} %copy-done.3, ...), custom_call_target="tpu_custom_call" | custom-call | tf_op jit(solution)/shard_map/step/pallas_call | solution.py:392
  62.5 8.4 %all-to-all-start.4 = ((bf16[16,16,640]{2,1,0:T(8,128)(2,1)}), bf16[16,16,640]{2,1,0:T(8,128)(2,1)S(1)}, u32[]{:S(2)}, u32[]{:S(2)}) async-start(bf16[16,16,640]{2,1,0:T(8,128)(2,1)} %get-tuple-element.24), calls=%async_computation.4 | async-start | bytes 655360 | tf_op jit(solution)/shard_map/all_to_all | solution.py:405
  70.9 2.7 %scan.1 = (f32[128,512]{1,0:T(8,128)S(1)}, f32[128,512]{1,0:T(8,128)S(1)}, f32[8,16,512]{2,1,0:T(8,128)S(1)}, f32[8,512]{1,0:T(8,128)S(1)}) custom-call(f32[144,512]{1,0:T(8,128)S(1)} %get-tuple-element.25.step_ref, f32[128,512]{1,0:T(8,128)S(1)} %get-tuple-element.26.u_ref, f32[128,128]{1,0:T(8,128)S(1)} %get-tuple-element.27.bc_ref, ...), custom_call_target="tpu_custom_call" | custom-call | tf_op jit(solution)/shard_map/scan/pallas_call | solution.py:406
  73.6 6.8 %all-to-all-done.4.got_ref = bf16[16,16,640]{2,1,0:T(8,128)(2,1)S(1)} async-done(((bf16[16,16,640]{2,1,0:T(8,128)(2,1)}), bf16[16,16,640]{2,1,0:T(8,128)(2,1)S(1)}, u32[]{:S(2)}, u32[]{:S(2)}) %all-to-all-start.4) | async-done | bytes 327712 | tf_op jit(solution)/shard_map/all_to_all | solution.py:405
  80.4 1.8 %finish.1 = (bf16[128,512]{1,0:T(8,128)(2,1)}, bf16[4,2,512]{2,1,0:T(2,128)(2,1)}) custom-call(bf16[16,16,640]{2,1,0:T(8,128)(2,1)S(1)} %all-to-all-done.4.got_ref, f32[128,512]{1,0:T(8,128)S(1)} %get-tuple-element.30.y_ref, f32[128,512]{1,0:T(8,128)S(1)} %get-tuple-element.31.reach_ref, f32[128,128]{1,0:T(8,128)S(1)} %get-tuple-element.27.bc_ref, ...), custom_call_target="tpu_custom_call" | custom-call | tf_op jit(solution)/shard_map/finish/pallas_call | solution.py:417
  (18 shorter events, 0.1 us)
Async XLA Ops:
  0.6 11.8 %copy-start.2 = (bf16[128,512]{1,0:T(8,128)(2,1)S(1)}, bf16[128,512]{1,0:T(8,128)(2,1)}, u32[]{:S(2)}) copy-start(bf16[128,512]{1,0:T(8,128)(2,1)} %x_ref.3) | copy-start | bytes 393220
  2.1 10.4 %copy-start.5 = (f32[512,16]{0,1:T(8,128)S(1)}, f32[512,16]{0,1:T(8,128)}, u32[]{:S(2)}) copy-start(f32[512,16]{0,1:T(8,128)} %param.19) | copy-start | bytes 98308
  2.1 10.4 %copy-start.6 = (bf16[4,2,512]{2,1,0:T(2,128)(2,1)S(1)}, bf16[4,2,512]{2,1,0:T(2,128)(2,1)}, u32[]{:S(2)}) copy-start(bf16[4,2,512]{2,1,0:T(2,128)(2,1)} %dz_ref.1) | copy-start | bytes 24580
  2.1 10.4 %copy-start.8 = (bf16[4,512]{1,0:T(4,128)(2,1)S(1)}, bf16[4,512]{1,0:T(4,128)(2,1)}, u32[]{:S(2)}) copy-start(bf16[4,512]{1,0:T(4,128)(2,1)} %w_ref.1) | copy-start | bytes 12292
  2.1 10.4 %copy-start.10 = (f32[512]{0:T(512)S(1)}, f32[512]{0:T(512)}, u32[]{:S(2)}) copy-start(f32[512]{0:T(512)} %skip_ref.1) | copy-start | bytes 6148
  2.1 17.7 %all-to-all-start = ((bf16[16,3,512]{2,1,0:T(4,128)(2,1)}), bf16[16,3,512]{2,1,0:T(4,128)(2,1)S(1)}, u32[]{:S(2)}, u32[]{:S(2)}) async-start(bf16[16,3,512]{2,1,0:T(4,128)(2,1)} %broadcast_in_dim.2), calls=%async_computation | async-start | bytes 131072 | tf_op jit(solution)/shard_map/all_to_all | solution.py:348
  12.4 0.7 copy-start.9
  12.4 0.7 copy-start.11
  12.4 0.7 copy-start.12
  13.1 1.1 %copy-start = (bf16[512,544]{0,1:T(8,128)(2,1)S(1)}, bf16[512,544]{0,1:T(8,128)(2,1)}, u32[]{:S(2)}) copy-start(bf16[512,544]{0,1:T(8,128)(2,1)} %param.16) | copy-start | bytes 1671172
  14.1 0.9 %copy-start.4 = (bf16[128,512]{1,0:T(8,128)(2,1)S(1)}, bf16[128,512]{1,0:T(8,128)(2,1)}, u32[]{:S(2)}) copy-start(bf16[128,512]{1,0:T(8,128)(2,1)} %z_ref.1) | copy-start | bytes 393220
  15.0 4.8 %copy-start.1 = (bf16[512,544]{0,1:T(8,128)(2,1)S(1)}, bf16[512,544]{0,1:T(8,128)(2,1)}, u32[]{:S(2)}) copy-start(bf16[512,544]{0,1:T(8,128)(2,1)} %param.16) | copy-start | bytes 1671172
  15.0 4.8 %copy-start.7 = (bf16[4,2,512]{2,1,0:T(2,128)(2,1)S(1)}, bf16[4,2,512]{2,1,0:T(2,128)(2,1)}, u32[]{:S(2)}) copy-start(bf16[4,2,512]{2,1,0:T(2,128)(2,1)} %dx_ref.1) | copy-start | bytes 24580
  30.3 29.9 %copy-start.3 = (bf16[512,512]{1,0:T(8,128)(2,1)S(1)}, bf16[512,512]{1,0:T(8,128)(2,1)}, u32[]{:S(2)}) copy-start(bf16[512,512]{1,0:T(8,128)(2,1)} %dtw_ref.1) | copy-start | bytes 1572868
  62.5 17.9 %all-to-all-start.4 = ((bf16[16,16,640]{2,1,0:T(8,128)(2,1)}), bf16[16,16,640]{2,1,0:T(8,128)(2,1)S(1)}, u32[]{:S(2)}, u32[]{:S(2)}) async-start(bf16[16,16,640]{2,1,0:T(8,128)(2,1)} %get-tuple-element.24), calls=%async_computation.4 | async-start | bytes 655360 | tf_op jit(solution)/shard_map/all_to_all | solution.py:405

commit v4 on v3

--- a/solution.py
+++ b/solution.py
@@ -200,8 +200,9 @@
     total = left[0:1] + step[0:1]
     coarse = jnp.concatenate([total[:, 128 * k : 128 * k + 128] for k in range(width // 128)], 0)
     fine = coarse - coarse.astype(BF16).astype(F32)
-    side = jnp.concatenate([coarse, fine, jnp.zeros((8, 128), F32)], 0)
-    result = jnp.concatenate([jnp.concatenate(ends, 0), side], 1).astype(BF16)
+    ends = jnp.concatenate(ends, 0)
+    side = jnp.concatenate([coarse, fine], 0)
+    result = jnp.concatenate([ends[:8], ends[8:], side], 1).astype(BF16)
     for k in range(msg_ref.shape[0]):
         msg_ref[k] = result
 
@@ -268,10 +269,12 @@
             r = p * BLOCKS + k
             if k > 0:
                 incoming = jnp.where((mine == p) & (position == k), h, incoming)
-            side = got_ref[r, :, width:].astype(F32)
+            block = got_ref[r].astype(F32)
+            side = block[:, 2 * width :]
             total = side[0:4] + side[4:8]
             total = jnp.concatenate([total[i : i + 1] for i in range(4)], 1)
-            h = jnp.exp(nrate * total) * h + got_ref[r, :, :width].astype(F32)
+            end = jnp.concatenate([block[:, :width], block[:, width : 2 * width]], 0)
+            h = jnp.exp(nrate * total) * h + end
         finals.append(h)
     in_ref[...] = incoming
 
@@ -392,7 +395,7 @@
     send, step, bc, u, dbc = call(
         step_kernel,
         (
-            shape(places, N, width + 128, kind=BF16),
+            shape(places, N // 2, 2 * width + 128, kind=BF16),
             shape(rows + 16, width),
             shape(rows, 128),
             shape(rows, width),

time: 82.8 us -> 82.4 us (level)
  no operation moved by 1% of the time
where the time goes in v4:
time: 82.4 us; the launch traced here: 81.9 us
  blocking collectives  39.9 us (48%)
  starting transfers between devices  18.7 us (23%)
  waiting for transfers between devices  10.3 us (12%)
  Pallas kernels  8.15 us (10%)
  local copies, waits for them, and re-layouts  4.03 us (5%)
    all_to_all x1, blocking collectives, local(): got = lax.all_to_all(sums, 'tensor', 0, 0, axis_index_groups=far)  19.3 us
    all_to_all x1, blocking collectives, local(): everything = lax.all_to_all(sums, 'tensor', 0, 0, axis_index_groups=near)  10.4 us
    all_to_all x1, starting transfers between devices, local(): lax.all_to_all(jnp.broadcast_to(tail[None], (places, taps - 1, width)), '...  10.3 us
    all_to_all x1, blocking collectives, local(): got = lax.all_to_all(part, 'tensor', 0, 0, axis_index_groups=near)  10.2 us
    all_to_all x1, starting transfers between devices, local(): states = lax.all_to_all(send, 'group', 0, 0)  8.41 us
    all_to_all x1, waiting for transfers between devices, local(): states = lax.all_to_all(send, 'group', 0, 0)  6.54 us
    all_to_all x1, waiting for transfers between devices, local(): lax.all_to_all(jnp.broadcast_to(tail[None], (places, taps - 1, width)), '...  3.77 us
    pallas_call x1, Pallas kernels, local(): call(scan_kernel, (shape(rows, width), shape(rows, width), shape(2 * STEP...  2.66 us
  transfers between devices with their start and end apart: 2, of which 2 were waited for; matrix products, arithmetic and copies ran while one was open for 0% of the time, Pallas kernels for 4%

profile of v4, /device:TPU:1, one launch (start us, length us, event | category | flops | bytes accessed | tf_op | source)
XLA Modules:
  0.0 81.9 jit_solution(13423786082456430332)
XLA Ops:
  0.6 0.0 copy-start.2
  0.6 0.8 slice.3
  1.4 0.7 broadcast_in_dim.2
  2.1 10.3 %all-to-all-start = ((bf16[16,3,512]{2,1,0:T(4,128)(2,1)}), bf16[16,3,512]{2,1,0:T(4,128)(2,1)S(1)}, u32[]{:S(2)}, u32[]{:S(2)}) async-start(bf16[16,3,512]{2,1,0:T(4,128)(2,1)} %broadcast_in_dim.2), calls=%async_computation | async-start | bytes 131072 | tf_op jit(solution)/shard_map/all_to_all | solution.py:351
  12.4 0.0 copy-start.11
  12.4 0.0 copy-start.12
  12.5 0.6 copy-done.9
  13.1 0.0 copy-done.11
  13.1 1.1 %copy-done = bf16[512,544]{0,1:T(8,128)(2,1)S(1)} copy-done((bf16[512,544]{0,1:T(8,128)(2,1)S(1)}, bf16[512,544]{0,1:T(8,128)(2,1)}, u32[]{:S(2)}) %copy-start) | copy-done | bytes 557080
  14.1 0.9 %copy-done.4 = bf16[128,512]{1,0:T(8,128)(2,1)S(1)} copy-done((bf16[128,512]{1,0:T(8,128)(2,1)S(1)}, bf16[128,512]{1,0:T(8,128)(2,1)}, u32[]{:S(2)}) %copy-start.4) | copy-done | bytes 131096
  15.0 1.0 %prepare.1 = (f32[128,640]{1,0:T(8,128)S(1)}, bf16[128,512]{1,0:T(8,128)(2,1)S(1)}, f32[16,512]{1,0:T(8,128)S(1)}, f32[128,512]{1,0:T(8,128)S(1)}, f32[24,512]{1,0:T(8,128)S(1)}) custom-call(s32[2]{0:T(128)S(1)} %copy-done.12, bf16[128,512]{1,0:T(8,128)(2,1)S(1)} %copy-done.2, bf16[4,512]{1,0:T(4,128)(2,1)S(1)} %copy-done.8, bf16[512]{0:T(512)(128)(2,1)S(1)} %copy-done.11, ...), custom_call_target="tpu_custom_call" | custom-call | tf_op jit(solution)/shard_map/prepare/pallas_call | solution.py:355
  16.0 3.8 %all-to-all-done.tails_ref = bf16[16,3,512]{2,1,0:T(4,128)(2,1)S(1)} async-done(((bf16[16,3,512]{2,1,0:T(4,128)(2,1)}), bf16[16,3,512]{2,1,0:T(4,128)(2,1)S(1)}, u32[]{:S(2)}, u32[]{:S(2)}) %all-to-all-start) | async-done | bytes 49184 | tf_op jit(solution)/shard_map/all_to_all | solution.py:351
  19.8 0.0 copy-done.7
  19.8 0.3 project.1
  20.2 10.2 %all_to_all.25.got_ref = bf16[8,16,640]{2,1,0:T(8,128)(2,1)S(1)} all-to-all(bf16[8,16,640]{2,1,0:T(8,128)(2,1)S(1)} %get-tuple-element.21), channel_id=1, replica_groups={{0,1,2,3,4,5,6,7},{10,11,12,13,14,15,8,9},{20,21,22,23,16,17,18,19},{30..., dimensions={0} | all-to-all | bytes 327680 | tf_op jit(solution)/shard_map/all_to_all | solution.py:387
  30.4 19.3 %all_to_all.26.got_ref = bf16[4,16,640]{2,1,0:T(8,128)(2,1)S(1)} all-to-all(bf16[4,16,640]{2,1,0:T(8,128)(2,1)S(1)} %near_sum.1), channel_id=1, replica_groups={{0,10,20,30},{1,11,21,31},{2,12,22,24},{3,13,23,25},{4,14,16,26},{5,15,..., dimensions={0} | all-to-all | bytes 163840 | tf_op jit(solution)/shard_map/all_to_all | solution.py:391
  49.7 0.1 far_sum.1
  49.8 10.4 %all_to_all.27.all_ref = bf16[8,16,640]{2,1,0:T(8,128)(2,1)S(1)} all-to-all(bf16[8,16,640]{2,1,0:T(8,128)(2,1)S(1)} %far_sum.1), channel_id=1, replica_groups={{0,1,2,3,4,5,6,7},{10,11,12,13,14,15,8,9},{20,21,22,23,16,17,18,19},{30..., dimensions={0} | all-to-all | bytes 327680 | tf_op jit(solution)/shard_map/all_to_all | solution.py:393
  60.2 0.0 copy-done.3
  60.2 2.3 %step.1 = (bf16[16,8,1152]{2,1,0:T(8,128)(2,1)}, f32[144,512]{1,0:T(8,128)S(1)}, f32[128,128]{1,0:T(8,128)S(1)}, f32[128,512]{1,0:T(8,128)S(1)}, f32[8,128]{1,0:T(8,128)S(1)}) custom-call(bf16[8,16,640]{2,1,0:T(8,128)(2,1)S(1)} %all_to_all.27.all_ref, bf16[144,512]{1,0:T(8,128)(2,1)S(1)} %get-tuple-element.22.cin_ref, bf16[512,512]{1,0:T(8,128)(2,1)S(1)} %copy-done.3, ...), custom_call_target="tpu_custom_call" | custom-call | tf_op jit(solution)/shard_map/step/pallas_call | solution.py:395
  62.5 8.4 %all-to-all-start.4 = ((bf16[16,8,1152]{2,1,0:T(8,128)(2,1)}), bf16[16,8,1152]{2,1,0:T(8,128)(2,1)S(1)}, u32[]{:S(2)}, u32[]{:S(2)}) async-start(bf16[16,8,1152]{2,1,0:T(8,128)(2,1)} %get-tuple-element.24), calls=%async_computation.4 | async-start | bytes 589824 | tf_op jit(solution)/shard_map/all_to_all | solution.py:408
  70.9 2.7 %scan.1 = (f32[128,512]{1,0:T(8,128)S(1)}, f32[128,512]{1,0:T(8,128)S(1)}, f32[8,16,512]{2,1,0:T(8,128)S(1)}, f32[8,512]{1,0:T(8,128)S(1)}) custom-call(f32[144,512]{1,0:T(8,128)S(1)} %get-tuple-element.25.step_ref, f32[128,512]{1,0:T(8,128)S(1)} %get-tuple-element.26.u_ref, f32[128,128]{1,0:T(8,128)S(1)} %get-tuple-element.27.bc_ref, ...), custom_call_target="tpu_custom_call" | custom-call | tf_op jit(solution)/shard_map/scan/pallas_call | solution.py:409
  73.5 6.5 %all-to-all-done.4.got_ref = bf16[16,8,1152]{2,1,0:T(8,128)(2,1)S(1)} async-done(((bf16[16,8,1152]{2,1,0:T(8,128)(2,1)}), bf16[16,8,1152]{2,1,0:T(8,128)(2,1)S(1)}, u32[]{:S(2)}, u32[]{:S(2)}) %all-to-all-start.4) | async-done | bytes 294944 | tf_op jit(solution)/shard_map/all_to_all | solution.py:408
  80.1 1.8 %finish.1 = (bf16[128,512]{1,0:T(8,128)(2,1)}, bf16[4,2,512]{2,1,0:T(2,128)(2,1)}) custom-call(bf16[16,8,1152]{2,1,0:T(8,128)(2,1)S(1)} %all-to-all-done.4.got_ref, f32[128,512]{1,0:T(8,128)S(1)} %get-tuple-element.30.y_ref, f32[128,512]{1,0:T(8,128)S(1)} %get-tuple-element.31.reach_ref, f32[128,128]{1,0:T(8,128)S(1)} %get-tuple-element.27.bc_ref, ...), custom_call_target="tpu_custom_call" | custom-call | tf_op jit(solution)/shard_map/finish/pallas_call | solution.py:420
  (18 shorter events, 0.1 us)
Async XLA Ops:
  0.6 11.8 %copy-start.2 = (bf16[128,512]{1,0:T(8,128)(2,1)S(1)}, bf16[128,512]{1,0:T(8,128)(2,1)}, u32[]{:S(2)}) copy-start(bf16[128,512]{1,0:T(8,128)(2,1)} %x_ref.3) | copy-start | bytes 393220
  2.1 10.4 %copy-start.5 = (f32[512,16]{0,1:T(8,128)S(1)}, f32[512,16]{0,1:T(8,128)}, u32[]{:S(2)}) copy-start(f32[512,16]{0,1:T(8,128)} %param.19) | copy-start | bytes 98308
  2.1 10.4 %copy-start.6 = (bf16[4,2,512]{2,1,0:T(2,128)(2,1)S(1)}, bf16[4,2,512]{2,1,0:T(2,128)(2,1)}, u32[]{:S(2)}) copy-start(bf16[4,2,512]{2,1,0:T(2,128)(2,1)} %dz_ref.1) | copy-start | bytes 24580
  2.1 10.4 %copy-start.8 = (bf16[4,512]{1,0:T(4,128)(2,1)S(1)}, bf16[4,512]{1,0:T(4,128)(2,1)}, u32[]{:S(2)}) copy-start(bf16[4,512]{1,0:T(4,128)(2,1)} %w_ref.1) | copy-start | bytes 12292
  2.1 10.4 %copy-start.10 = (f32[512]{0:T(512)S(1)}, f32[512]{0:T(512)}, u32[]{:S(2)}) copy-start(f32[512]{0:T(512)} %skip_ref.1) | copy-start | bytes 6148
  2.1 17.7 %all-to-all-start = ((bf16[16,3,512]{2,1,0:T(4,128)(2,1)}), bf16[16,3,512]{2,1,0:T(4,128)(2,1)S(1)}, u32[]{:S(2)}, u32[]{:S(2)}) async-start(bf16[16,3,512]{2,1,0:T(4,128)(2,1)} %broadcast_in_dim.2), calls=%async_computation | async-start | bytes 131072 | tf_op jit(solution)/shard_map/all_to_all | solution.py:351
  12.4 0.7 copy-start.9
  12.4 0.7 copy-start.11
  12.4 0.7 copy-start.12
  13.1 1.1 %copy-start = (bf16[512,544]{0,1:T(8,128)(2,1)S(1)}, bf16[512,544]{0,1:T(8,128)(2,1)}, u32[]{:S(2)}) copy-start(bf16[512,544]{0,1:T(8,128)(2,1)} %param.16) | copy-start | bytes 1671172
  14.1 0.9 %copy-start.4 = (bf16[128,512]{1,0:T(8,128)(2,1)S(1)}, bf16[128,512]{1,0:T(8,128)(2,1)}, u32[]{:S(2)}) copy-start(bf16[128,512]{1,0:T(8,128)(2,1)} %z_ref.1) | copy-start | bytes 393220
  15.0 4.8 %copy-start.1 = (bf16[512,544]{0,1:T(8,128)(2,1)S(1)}, bf16[512,544]{0,1:T(8,128)(2,1)}, u32[]{:S(2)}) copy-start(bf16[512,544]{0,1:T(8,128)(2,1)} %param.16) | copy-start | bytes 1671172
  15.0 4.8 %copy-start.7 = (bf16[4,2,512]{2,1,0:T(2,128)(2,1)S(1)}, bf16[4,2,512]{2,1,0:T(2,128)(2,1)}, u32[]{:S(2)}) copy-start(bf16[4,2,512]{2,1,0:T(2,128)(2,1)} %dx_ref.1) | copy-start | bytes 24580
  30.3 29.9 %copy-start.3 = (bf16[512,512]{1,0:T(8,128)(2,1)S(1)}, bf16[512,512]{1,0:T(8,128)(2,1)}, u32[]{:S(2)}) copy-start(bf16[512,512]{1,0:T(8,128)(2,1)} %dtw_ref.1) | copy-start | bytes 1572868
  62.5 17.6 %all-to-all-start.4 = ((bf16[16,8,1152]{2,1,0:T(8,128)(2,1)}), bf16[16,8,1152]{2,1,0:T(8,128)(2,1)S(1)}, u32[]{:S(2)}, u32[]{:S(2)}) async-start(bf16[16,8,1152]{2,1,0:T(8,128)(2,1)} %get-tuple-element.24), calls=%async_computation.4 | async-start | bytes 589824 | tf_op jit(solution)/shard_map/all_to_all | solution.py:408

commit v5 on v4

--- a/solution.py
+++ b/solution.py
@@ -6,6 +6,7 @@
 from jax.sharding import PartitionSpec as P
 
 N = 16
+KEPT = 8
 R = 512
 STEPS = 4
 F32 = jnp.float32
@@ -162,7 +163,7 @@
 
 def step_kernel(
     all_ref, cin_ref, dtw_ref, small_ref, nrate_ref,
-    msg_ref, step_ref, bc_ref, u_ref, dbc_ref, low_ref, left_ref,
+    msg_ref, step_ref, bc_ref, dbc_ref, low_ref, left_ref, u_ref,
 ):
     rows, width = u_ref.shape
     lines, tiles = [], []
@@ -208,16 +209,27 @@
 
 
 def scan_kernel(
-    step_ref, u_ref, bc_ref, cin_ref, gate_ref, small_ref, nrate_ref, dbc_ref,
-    out_ref, reach_ref, from_ref, dout_ref,
+    step_ref, bc_ref, cin_ref, gate_ref, small_ref, nrate_ref, dbc_ref,
+    out_ref, reach_ref, carry_ref, from_ref, dout_ref, u_ref,
 ):
     rows, width = u_ref.shape
     down = lax.broadcasted_iota(jnp.int32, (rows, rows), 0)
     over = lax.broadcasted_iota(jnp.int32, (rows, rows), 1)
+    u_ref[...] = step_ref[0:rows, :] * cin_ref[0:rows, :].astype(F32)
     upto = jnp.where(over <= down, 1.0, 0.0).astype(BF16)
     reach_ref[...] = sum(
         jnp.dot(upto, part, preferred_element_type=F32) for part in parts(step_ref[0:rows, :])
     )
+
+    def carried(g, keep):
+        at = pl.ds(pl.multiple_of(16 * g, 16), 16)
+        reach = reach_ref[at, :]
+        for n in range(KEPT):
+            factor = jnp.exp(nrate_ref[n : n + 1, :] * reach)
+            carry_ref[n, at, :] = (bc_ref[at, N + n : N + n + 1] * factor).astype(BF16)
+        return keep
+
+    lax.fori_loop(0, rows // 16, carried, 0)
     dbc = jnp.transpose(jnp.concatenate([dbc_ref[...], jnp.zeros((120, 128), F32)], 0))
     nrate = nrate_ref[...]
     skip = small_ref[1:2, :]
@@ -248,13 +260,13 @@
         kept[s] = decay * kept[s]
         state[s] = decay * state[s] + dbc[0:N, r : r + 1] * (d * dec[r : r + 1])
         c = dbc[N : 2 * N, r : r + 1]
-        from_ref[r] = c * kept[s]
+        from_ref[r] = (c * kept[s]).astype(BF16)
         own.append(jnp.sum(c * state[s], axis=0, keepdims=True))
     dout_ref[...] = jnp.concatenate(own, 0) + skip * dec[0 : 2 * STEPS]
 
 
 def finish_kernel(
-    got_ref, y_ref, reach_ref, bc_ref, gate_ref, nrate_ref, small_ref, from_ref, own_ref,
+    got_ref, y_ref, reach_ref, carry_ref, bc_ref, gate_ref, nrate_ref, small_ref, from_ref, own_ref,
     out_ref, dec_ref, in_ref,
 ):
     rows, width = y_ref.shape
@@ -283,7 +295,9 @@
         s = reach_ref[at, :]
         c = bc_ref[at, :]
         acc = jnp.zeros((16, width), F32)
-        for n in range(N):
+        for n in range(KEPT):
+            acc = acc + in_ref[n : n + 1, :] * carry_ref[n, at, :].astype(F32)
+        for n in range(KEPT, N):
             acc = acc + c[:, N + n : N + n + 1] * (
                 in_ref[n : n + 1, :] * jnp.exp(nrate_ref[n : n + 1, :] * s)
             )
@@ -296,7 +310,7 @@
     ]
     for t in range(STEPS):
         pair = [
-            jnp.sum(from_ref[2 * t + s] * states[s], axis=0, keepdims=True) for s in range(2)
+            jnp.sum(from_ref[2 * t + s].astype(F32) * states[s], axis=0, keepdims=True) for s in range(2)
         ]
         at = slice(2 * t, 2 * t + 2)
         value = (jnp.concatenate(pair, 0) + own_ref[at, :]) * small_ref[8 + 2 * t : 10 + 2 * t, :]
@@ -392,38 +406,43 @@
     sums = call(far_sum_kernel, shape(NEAR, 16, WIDE, kind=BF16), inputs=1, name="far_sum")(got)
     everything = lax.all_to_all(sums, "tensor", 0, 0, axis_index_groups=near)
 
-    send, step, bc, u, dbc = call(
+    send, step, bc, dbc = call(
         step_kernel,
         (
             shape(places, N // 2, 2 * width + 128, kind=BF16),
             shape(rows + 16, width),
             shape(rows, 128),
-            shape(rows, width),
             shape(8, 128),
         ),
-        [pltpu.VMEM((rows + 16, R), BF16), pltpu.VMEM((rows, width), F32)],
+        [
+            pltpu.VMEM((rows + 16, R), BF16),
+            pltpu.VMEM((rows, width), F32),
+            pltpu.VMEM((rows, width), F32),
+        ],
         inputs=5,
         name="step",
     )(everything, cin, dtproj_weight, small, nrate)
     states = lax.all_to_all(send, "group", 0, 0)
-    y, reach, share, own = call(
+    y, reach, carry, share, own = call(
         scan_kernel,
         (
             shape(rows, width),
             shape(rows, width),
-            shape(2 * STEPS, N, width),
+            shape(KEPT, rows, width, kind=BF16),
+            shape(2 * STEPS, N, width, kind=BF16),
             shape(2 * STEPS, width),
         ),
-        inputs=8,
+        [pltpu.VMEM((rows, width), F32)],
+        inputs=7,
         name="scan",
-    )(step, u, bc, cin, gate, small, nrate, dbc)
+    )(step, bc, cin, gate, small, nrate, dbc)
     return call(
         finish_kernel,
         (shape(rows, width, kind=BF16), shape(STEPS, 2, width, kind=BF16)),
         [pltpu.VMEM((N, width), F32)],
-        inputs=9,
+        inputs=10,
         name="finish",
-    )(states, y, reach, bc, gate, nrate, small, share, own)
+    )(states, y, reach, carry, bc, gate, nrate, small, share, own)
 
 
 def solution(mesh):

time: 82.4 us -> 82.2 us (level)
  waiting for transfers between devices: 10.3 us -> 9.47 us
    all_to_all x1, waiting for transfers between devices: 6.54 us -> 5.71 us  [local(): states = lax.all_to_all(send, 'group', 0, 0)]
    pallas_call x1, Pallas kernels: 2.66 us -> 3.5 us  [local(): call(scan_kernel, (shape(rows, width), shape(rows, width), shape(KEPT, ro...]
  transfers between devices with their start and end apart: 2 -> 2, of which waited for: 2 -> 2; matrix products, arithmetic and copies ran while one was open for 0% -> 0% of each run, Pallas kernels for 4% -> 5%
where the time goes in v5:
time: 82.2 us; the launch traced here: 81.7 us
  blocking collectives  39.9 us (49%)
  starting transfers between devices  18.7 us (23%)
  waiting for transfers between devices  9.47 us (12%)
  Pallas kernels  8.78 us (11%)
  local copies, waits for them, and re-layouts  4.03 us (5%)
    all_to_all x1, blocking collectives, local(): got = lax.all_to_all(sums, 'tensor', 0, 0, axis_index_groups=far)  19.3 us
    all_to_all x1, blocking collectives, local(): everything = lax.all_to_all(sums, 'tensor', 0, 0, axis_index_groups=near)  10.4 us
    all_to_all x1, starting transfers between devices, local(): lax.all_to_all(jnp.broadcast_to(tail[None], (places, taps - 1, width)), '...  10.3 us
    all_to_all x1, blocking collectives, local(): got = lax.all_to_all(part, 'tensor', 0, 0, axis_index_groups=near)  10.2 us
    all_to_all x1, starting transfers between devices, local(): states = lax.all_to_all(send, 'group', 0, 0)  8.41 us
    all_to_all x1, waiting for transfers between devices, local(): states = lax.all_to_all(send, 'group', 0, 0)  5.71 us
    all_to_all x1, waiting for transfers between devices, local(): lax.all_to_all(jnp.broadcast_to(tail[None], (places, taps - 1, width)), '...  3.77 us
    pallas_call x1, Pallas kernels, local(): call(scan_kernel, (shape(rows, width), shape(rows, width), shape(KEPT, ro...  3.5 us
  transfers between devices with their start and end apart: 2, of which 2 were waited for; matrix products, arithmetic and copies ran while one was open for 0% of the time, Pallas kernels for 5%

profile of v5, /device:TPU:1, one launch (start us, length us, event | category | flops | bytes accessed | tf_op | source)
XLA Modules:
  0.0 81.7 jit_solution(9254003102906307261)
XLA Ops:
  0.6 0.0 copy-start.2
  0.6 0.8 slice.3
  1.4 0.7 broadcast_in_dim.2
  2.1 10.3 %all-to-all-start = ((bf16[16,3,512]{2,1,0:T(4,128)(2,1)}), bf16[16,3,512]{2,1,0:T(4,128)(2,1)S(1)}, u32[]{:S(2)}, u32[]{:S(2)}) async-start(bf16[16,3,512]{2,1,0:T(4,128)(2,1)} %broadcast_in_dim.2), calls=%async_computation | async-start | bytes 131072 | tf_op jit(solution)/shard_map/all_to_all | solution.py:365
  12.4 0.0 copy-start.11
  12.4 0.0 copy-start.12
  12.5 0.6 copy-done.9
  13.1 0.0 copy-done.11
  13.1 1.1 %copy-done = bf16[512,544]{0,1:T(8,128)(2,1)S(1)} copy-done((bf16[512,544]{0,1:T(8,128)(2,1)S(1)}, bf16[512,544]{0,1:T(8,128)(2,1)}, u32[]{:S(2)}) %copy-start) | copy-done | bytes 557080
  14.1 0.9 %copy-done.4 = bf16[128,512]{1,0:T(8,128)(2,1)S(1)} copy-done((bf16[128,512]{1,0:T(8,128)(2,1)S(1)}, bf16[128,512]{1,0:T(8,128)(2,1)}, u32[]{:S(2)}) %copy-start.4) | copy-done | bytes 131096
  15.0 1.0 %prepare.1 = (f32[128,640]{1,0:T(8,128)S(1)}, bf16[128,512]{1,0:T(8,128)(2,1)S(1)}, f32[16,512]{1,0:T(8,128)S(1)}, f32[128,512]{1,0:T(8,128)S(1)}, f32[24,512]{1,0:T(8,128)S(1)}) custom-call(s32[2]{0:T(128)S(1)} %copy-done.12, bf16[128,512]{1,0:T(8,128)(2,1)S(1)} %copy-done.2, bf16[4,512]{1,0:T(4,128)(2,1)S(1)} %copy-done.8, bf16[512]{0:T(512)(128)(2,1)S(1)} %copy-done.11, ...), custom_call_target="tpu_custom_call" | custom-call | tf_op jit(solution)/shard_map/prepare/pallas_call | solution.py:369
  16.0 3.8 %all-to-all-done.tails_ref = bf16[16,3,512]{2,1,0:T(4,128)(2,1)S(1)} async-done(((bf16[16,3,512]{2,1,0:T(4,128)(2,1)}), bf16[16,3,512]{2,1,0:T(4,128)(2,1)S(1)}, u32[]{:S(2)}, u32[]{:S(2)}) %all-to-all-start) | async-done | bytes 49184 | tf_op jit(solution)/shard_map/all_to_all | solution.py:365
  19.8 0.0 copy-done.7
  19.8 0.3 project.1
  20.2 10.2 %all_to_all.25.got_ref = bf16[8,16,640]{2,1,0:T(8,128)(2,1)S(1)} all-to-all(bf16[8,16,640]{2,1,0:T(8,128)(2,1)S(1)} %get-tuple-element.21), channel_id=1, replica_groups={{0,1,2,3,4,5,6,7},{10,11,12,13,14,15,8,9},{20,21,22,23,16,17,18,19},{30..., dimensions={0} | all-to-all | bytes 327680 | tf_op jit(solution)/shard_map/all_to_all | solution.py:401
  30.4 19.3 %all_to_all.26.got_ref = bf16[4,16,640]{2,1,0:T(8,128)(2,1)S(1)} all-to-all(bf16[4,16,640]{2,1,0:T(8,128)(2,1)S(1)} %near_sum.1), channel_id=1, replica_groups={{0,10,20,30},{1,11,21,31},{2,12,22,24},{3,13,23,25},{4,14,16,26},{5,15,..., dimensions={0} | all-to-all | bytes 163840 | tf_op jit(solution)/shard_map/all_to_all | solution.py:405
  49.7 0.1 far_sum.1
  49.8 10.4 %all_to_all.27.all_ref = bf16[8,16,640]{2,1,0:T(8,128)(2,1)S(1)} all-to-all(bf16[8,16,640]{2,1,0:T(8,128)(2,1)S(1)} %far_sum.1), channel_id=1, replica_groups={{0,1,2,3,4,5,6,7},{10,11,12,13,14,15,8,9},{20,21,22,23,16,17,18,19},{30..., dimensions={0} | all-to-all | bytes 327680 | tf_op jit(solution)/shard_map/all_to_all | solution.py:407
  60.2 0.0 copy-done.3
  60.2 2.2 %step.1 = (bf16[16,8,1152]{2,1,0:T(8,128)(2,1)}, f32[144,512]{1,0:T(8,128)S(1)}, f32[128,128]{1,0:T(8,128)S(1)}, f32[8,128]{1,0:T(8,128)S(1)}) custom-call(bf16[8,16,640]{2,1,0:T(8,128)(2,1)S(1)} %all_to_all.27.all_ref, bf16[144,512]{1,0:T(8,128)(2,1)S(1)} %get-tuple-element.22.cin_ref, bf16[512,512]{1,0:T(8,128)(2,1)S(1)} %copy-done.3, ...), custom_call_target="tpu_custom_call" | custom-call | tf_op jit(solution)/shard_map/step/pallas_call | solution.py:409
  62.5 8.4 %all-to-all-start.4 = ((bf16[16,8,1152]{2,1,0:T(8,128)(2,1)}), bf16[16,8,1152]{2,1,0:T(8,128)(2,1)S(1)}, u32[]{:S(2)}, u32[]{:S(2)}) async-start(bf16[16,8,1152]{2,1,0:T(8,128)(2,1)} %get-tuple-element.24), calls=%async_computation.4 | async-start | bytes 589824 | tf_op jit(solution)/shard_map/all_to_all | solution.py:425
  70.9 3.5 %scan.1 = (f32[128,512]{1,0:T(8,128)S(1)}, f32[128,512]{1,0:T(8,128)S(1)}, bf16[8,128,512]{2,1,0:T(8,128)(2,1)S(1)}, bf16[8,16,512]{2,1,0:T(8,128)(2,1)S(1)}, f32[8,512]{1,0:T(8,128)S(1)}) custom-call(f32[144,512]{1,0:T(8,128)S(1)} %get-tuple-element.25.step_ref, f32[128,128]{1,0:T(8,128)S(1)} %get-tuple-element.26.bc_ref, ...), custom_call_target="tpu_custom_call" | custom-call | tf_op jit(solution)/shard_map/scan/pallas_call | solution.py:426
  74.4 5.7 %all-to-all-done.4.got_ref = bf16[16,8,1152]{2,1,0:T(8,128)(2,1)S(1)} async-done(((bf16[16,8,1152]{2,1,0:T(8,128)(2,1)}), bf16[16,8,1152]{2,1,0:T(8,128)(2,1)S(1)}, u32[]{:S(2)}, u32[]{:S(2)}) %all-to-all-start.4) | async-done | bytes 294944 | tf_op jit(solution)/shard_map/all_to_all | solution.py:425
  80.1 1.6 %finish.1 = (bf16[128,512]{1,0:T(8,128)(2,1)}, bf16[4,2,512]{2,1,0:T(2,128)(2,1)}) custom-call(bf16[16,8,1152]{2,1,0:T(8,128)(2,1)S(1)} %all-to-all-done.4.got_ref, f32[128,512]{1,0:T(8,128)S(1)} %get-tuple-element.29.y_ref, f32[128,512]{1,0:T(8,128)S(1)} %get-tuple-element.30.reach_ref, bf16[8,128,512]{2,1,0:T(8,128)(2,1)S(1)} %get-tuple-element.31.carry_ref, ...), custom_call_target="tpu_custom_call" | custom-call | tf_op jit(solution)/shard_map/finish/pallas_call | solution.py:439
  (18 shorter events, 0.1 us)
Async XLA Ops:
  0.6 11.8 %copy-start.2 = (bf16[128,512]{1,0:T(8,128)(2,1)S(1)}, bf16[128,512]{1,0:T(8,128)(2,1)}, u32[]{:S(2)}) copy-start(bf16[128,512]{1,0:T(8,128)(2,1)} %x_ref.3) | copy-start | bytes 393220
  2.1 10.4 %copy-start.5 = (f32[512,16]{0,1:T(8,128)S(1)}, f32[512,16]{0,1:T(8,128)}, u32[]{:S(2)}) copy-start(f32[512,16]{0,1:T(8,128)} %param.19) | copy-start | bytes 98308
  2.1 10.4 %copy-start.6 = (bf16[4,2,512]{2,1,0:T(2,128)(2,1)S(1)}, bf16[4,2,512]{2,1,0:T(2,128)(2,1)}, u32[]{:S(2)}) copy-start(bf16[4,2,512]{2,1,0:T(2,128)(2,1)} %dz_ref.1) | copy-start | bytes 24580
  2.1 10.4 %copy-start.8 = (bf16[4,512]{1,0:T(4,128)(2,1)S(1)}, bf16[4,512]{1,0:T(4,128)(2,1)}, u32[]{:S(2)}) copy-start(bf16[4,512]{1,0:T(4,128)(2,1)} %w_ref.1) | copy-start | bytes 12292
  2.1 10.4 %copy-start.10 = (f32[512]{0:T(512)S(1)}, f32[512]{0:T(512)}, u32[]{:S(2)}) copy-start(f32[512]{0:T(512)} %skip_ref.1) | copy-start | bytes 6148
  2.1 17.7 %all-to-all-start = ((bf16[16,3,512]{2,1,0:T(4,128)(2,1)}), bf16[16,3,512]{2,1,0:T(4,128)(2,1)S(1)}, u32[]{:S(2)}, u32[]{:S(2)}) async-start(bf16[16,3,512]{2,1,0:T(4,128)(2,1)} %broadcast_in_dim.2), calls=%async_computation | async-start | bytes 131072 | tf_op jit(solution)/shard_map/all_to_all | solution.py:365
  12.4 0.7 copy-start.9
  12.4 0.7 copy-start.11
  12.4 0.7 copy-start.12
  13.1 1.1 %copy-start = (bf16[512,544]{0,1:T(8,128)(2,1)S(1)}, bf16[512,544]{0,1:T(8,128)(2,1)}, u32[]{:S(2)}) copy-start(bf16[512,544]{0,1:T(8,128)(2,1)} %param.16) | copy-start | bytes 1671172
  14.1 0.9 %copy-start.4 = (bf16[128,512]{1,0:T(8,128)(2,1)S(1)}, bf16[128,512]{1,0:T(8,128)(2,1)}, u32[]{:S(2)}) copy-start(bf16[128,512]{1,0:T(8,128)(2,1)} %z_ref.1) | copy-start | bytes 393220
  15.0 4.8 %copy-start.1 = (bf16[512,544]{0,1:T(8,128)(2,1)S(1)}, bf16[512,544]{0,1:T(8,128)(2,1)}, u32[]{:S(2)}) copy-start(bf16[512,544]{0,1:T(8,128)(2,1)} %param.16) | copy-start | bytes 1671172
  15.0 4.8 %copy-start.7 = (bf16[4,2,512]{2,1,0:T(2,128)(2,1)S(1)}, bf16[4,2,512]{2,1,0:T(2,128)(2,1)}, u32[]{:S(2)}) copy-start(bf16[4,2,512]{2,1,0:T(2,128)(2,1)} %dx_ref.1) | copy-start | bytes 24580
  30.3 29.9 %copy-start.3 = (bf16[512,512]{1,0:T(8,128)(2,1)S(1)}, bf16[512,512]{1,0:T(8,128)(2,1)}, u32[]{:S(2)}) copy-start(bf16[512,512]{1,0:T(8,128)(2,1)} %dtw_ref.1) | copy-start | bytes 1572868
  62.5 17.6 %all-to-all-start.4 = ((bf16[16,8,1152]{2,1,0:T(8,128)(2,1)}), bf16[16,8,1152]{2,1,0:T(8,128)(2,1)S(1)}, u32[]{:S(2)}, u32[]{:S(2)}) async-start(bf16[16,8,1152]{2,1,0:T(8,128)(2,1)} %get-tuple-element.24), calls=%async_computation.4 | async-start | bytes 589824 | tf_op jit(solution)/shard_map/all_to_all | solution.py:425

commit v6 on v5

--- a/solution.py
+++ b/solution.py
@@ -74,7 +74,7 @@
     cin_ref[...] = cin
     part_ref[:, : R + 2 * N] = onto(cin, xw_ref)
     part_ref[:, R + 2 * N :] = jnp.zeros((rows, WIDE - R - 2 * N), F32)
-    nrate_ref[...] = -rate_ref[...]
+    nrate_ref[...] = rate_ref[...] * (-1.4426950408889634)
     gate_ref[...] = silu(z_ref[...].astype(F32))
     small_ref[0:8, :] = jnp.concatenate(
         [
@@ -196,7 +196,7 @@
         acc = jnp.zeros((16, width), F32)
         for g in range(rows // 16):
             at = slice(16 * g, 16 * g + 16)
-            acc = acc + jnp.exp(rate * left_ref[at, :]) * (bc_ref[at, n : n + 1] * u_ref[at, :])
+            acc = acc + jnp.exp2(rate * left_ref[at, :]) * (bc_ref[at, n : n + 1] * u_ref[at, :])
         ends.append(jnp.sum(acc, axis=0, keepdims=True))
     total = left[0:1] + step[0:1]
     coarse = jnp.concatenate([total[:, 128 * k : 128 * k + 128] for k in range(width // 128)], 0)
@@ -225,7 +225,7 @@
         at = pl.ds(pl.multiple_of(16 * g, 16), 16)
         reach = reach_ref[at, :]
         for n in range(KEPT):
-            factor = jnp.exp(nrate_ref[n : n + 1, :] * reach)
+            factor = jnp.exp2(nrate_ref[n : n + 1, :] * reach)
             carry_ref[n, at, :] = (bc_ref[at, N + n : N + n + 1] * factor).astype(BF16)
         return keep
 
@@ -242,7 +242,7 @@
         u8 = u_ref[at, :]
         values = []
         for j in range(8):
-            h = jnp.exp(nrate * d8[j : j + 1]) * h + bc[0:N, j : j + 1] * u8[j : j + 1]
+            h = jnp.exp2(nrate * d8[j : j + 1]) * h + bc[0:N, j : j + 1] * u8[j : j + 1]
             values.append(jnp.sum(bc[N : 2 * N, j : j + 1] * h, axis=0, keepdims=True))
         out_ref[at, :] = jnp.concatenate(values, 0)
         return h, pltpu.roll(bc, 120, 1)
@@ -256,7 +256,7 @@
     for r in range(2 * STEPS):
         s = r % 2
         d = step_ref[rows + r : rows + r + 1, :]
-        decay = jnp.exp(nrate * d)
+        decay = jnp.exp2(nrate * d)
         kept[s] = decay * kept[s]
         state[s] = decay * state[s] + dbc[0:N, r : r + 1] * (d * dec[r : r + 1])
         c = dbc[N : 2 * N, r : r + 1]
@@ -286,7 +286,7 @@
             total = side[0:4] + side[4:8]
             total = jnp.concatenate([total[i : i + 1] for i in range(4)], 1)
             end = jnp.concatenate([block[:, :width], block[:, width : 2 * width]], 0)
-            h = jnp.exp(nrate * total) * h + end
+            h = jnp.exp2(nrate * total) * h + end
         finals.append(h)
     in_ref[...] = incoming
 
@@ -299,7 +299,7 @@
             acc = acc + in_ref[n : n + 1, :] * carry_ref[n, at, :].astype(F32)
         for n in range(KEPT, N):
             acc = acc + c[:, N + n : N + n + 1] * (
-                in_ref[n : n + 1, :] * jnp.exp(nrate_ref[n : n + 1, :] * s)
+                in_ref[n : n + 1, :] * jnp.exp2(nrate_ref[n : n + 1, :] * s)
             )
         out_ref[at, :] = (y_ref[at, :] + acc * gate_ref[at, :]).astype(BF16)
         return carry

time: 82.2 us -> 82.2 us (level)
  transfers between devices with their start and end apart: 2 -> 2, of which waited for: 2 -> 2; matrix products, arithmetic and copies ran while one was open for 0% -> 0% of each run, Pallas kernels for 5% -> 6%
where the time goes in v6:
time: 82.2 us; the launch traced here: 81.6 us
  blocking collectives  39.9 us (49%)
  starting transfers between devices  18.7 us (23%)
  waiting for transfers between devices  9.47 us (12%)
  Pallas kernels  8.73 us (11%)
  local copies, waits for them, and re-layouts  4.03 us (5%)
    all_to_all x1, blocking collectives, local(): got = lax.all_to_all(sums, 'tensor', 0, 0, axis_index_groups=far)  19.3 us
    all_to_all x1, blocking collectives, local(): everything = lax.all_to_all(sums, 'tensor', 0, 0, axis_index_groups=near)  10.4 us
    all_to_all x1, starting transfers between devices, local(): lax.all_to_all(jnp.broadcast_to(tail[None], (places, taps - 1, width)), '...  10.3 us
    all_to_all x1, blocking collectives, local(): got = lax.all_to_all(part, 'tensor', 0, 0, axis_index_groups=near)  10.2 us
    all_to_all x1, starting transfers between devices, local(): states = lax.all_to_all(send, 'group', 0, 0)  8.41 us
    all_to_all x1, waiting for transfers between devices, local(): states = lax.all_to_all(send, 'group', 0, 0)  5.7 us
    all_to_all x1, waiting for transfers between devices, local(): lax.all_to_all(jnp.broadcast_to(tail[None], (places, taps - 1, width)), '...  3.77 us
    pallas_call x1, Pallas kernels, local(): call(scan_kernel, (shape(rows, width), shape(rows, width), shape(KEPT, ro...  3.5 us
  transfers between devices with their start and end apart: 2, of which 2 were waited for; matrix products, arithmetic and copies ran while one was open for 0% of the time, Pallas kernels for 6%

profile of v6, /device:TPU:1, one launch (start us, length us, event | category | flops | bytes accessed | tf_op | source)
XLA Modules:
  0.0 81.6 jit_solution(4239816307290478228)
XLA Ops:
  0.6 0.8 slice.3
  1.4 0.7 broadcast_in_dim.2
  2.1 10.3 %all-to-all-start = ((bf16[16,3,512]{2,1,0:T(4,128)(2,1)}), bf16[16,3,512]{2,1,0:T(4,128)(2,1)S(1)}, u32[]{:S(2)}, u32[]{:S(2)}) async-start(bf16[16,3,512]{2,1,0:T(4,128)(2,1)} %broadcast_in_dim.2), calls=%async_computation | async-start | bytes 131072 | tf_op jit(solution)/shard_map/all_to_all | solution.py:365
  12.4 0.0 copy-start.11
  12.4 0.0 copy-start.12
  12.4 0.0 copy-done.2
  12.4 0.0 copy-done.5
  12.4 0.0 copy-done.6
  12.5 0.6 copy-done.9
  13.1 0.0 copy-done.11
  13.1 1.1 %copy-done = bf16[512,544]{0,1:T(8,128)(2,1)S(1)} copy-done((bf16[512,544]{0,1:T(8,128)(2,1)S(1)}, bf16[512,544]{0,1:T(8,128)(2,1)}, u32[]{:S(2)}) %copy-start) | copy-done | bytes 557080
  14.1 0.9 %copy-done.4 = bf16[128,512]{1,0:T(8,128)(2,1)S(1)} copy-done((bf16[128,512]{1,0:T(8,128)(2,1)S(1)}, bf16[128,512]{1,0:T(8,128)(2,1)}, u32[]{:S(2)}) %copy-start.4) | copy-done | bytes 131096
  15.0 1.0 %prepare.1 = (f32[128,640]{1,0:T(8,128)S(1)}, bf16[128,512]{1,0:T(8,128)(2,1)S(1)}, f32[16,512]{1,0:T(8,128)S(1)}, f32[128,512]{1,0:T(8,128)S(1)}, f32[24,512]{1,0:T(8,128)S(1)}) custom-call(s32[2]{0:T(128)S(1)} %copy-done.12, bf16[128,512]{1,0:T(8,128)(2,1)S(1)} %copy-done.2, bf16[4,512]{1,0:T(4,128)(2,1)S(1)} %copy-done.8, bf16[512]{0:T(512)(128)(2,1)S(1)} %copy-done.11, ...), custom_call_target="tpu_custom_call" | custom-call | tf_op jit(solution)/shard_map/prepare/pallas_call | solution.py:369
  16.0 3.8 %all-to-all-done.tails_ref = bf16[16,3,512]{2,1,0:T(4,128)(2,1)S(1)} async-done(((bf16[16,3,512]{2,1,0:T(4,128)(2,1)}), bf16[16,3,512]{2,1,0:T(4,128)(2,1)S(1)}, u32[]{:S(2)}, u32[]{:S(2)}) %all-to-all-start) | async-done | bytes 49184 | tf_op jit(solution)/shard_map/all_to_all | solution.py:365
  19.8 0.3 project.1
  20.2 10.2 %all_to_all.25.got_ref = bf16[8,16,640]{2,1,0:T(8,128)(2,1)S(1)} all-to-all(bf16[8,16,640]{2,1,0:T(8,128)(2,1)S(1)} %get-tuple-element.21), channel_id=1, replica_groups={{0,1,2,3,4,5,6,7},{10,11,12,13,14,15,8,9},{20,21,22,23,16,17,18,19},{30..., dimensions={0} | all-to-all | bytes 327680 | tf_op jit(solution)/shard_map/all_to_all | solution.py:401
  30.4 19.3 %all_to_all.26.got_ref = bf16[4,16,640]{2,1,0:T(8,128)(2,1)S(1)} all-to-all(bf16[4,16,640]{2,1,0:T(8,128)(2,1)S(1)} %near_sum.1), channel_id=1, replica_groups={{0,10,20,30},{1,11,21,31},{2,12,22,24},{3,13,23,25},{4,14,16,26},{5,15,..., dimensions={0} | all-to-all | bytes 163840 | tf_op jit(solution)/shard_map/all_to_all | solution.py:405
  49.7 0.1 far_sum.1
  49.8 10.4 %all_to_all.27.all_ref = bf16[8,16,640]{2,1,0:T(8,128)(2,1)S(1)} all-to-all(bf16[8,16,640]{2,1,0:T(8,128)(2,1)S(1)} %far_sum.1), channel_id=1, replica_groups={{0,1,2,3,4,5,6,7},{10,11,12,13,14,15,8,9},{20,21,22,23,16,17,18,19},{30..., dimensions={0} | all-to-all | bytes 327680 | tf_op jit(solution)/shard_map/all_to_all | solution.py:407
  60.2 2.2 %step.1 = (bf16[16,8,1152]{2,1,0:T(8,128)(2,1)}, f32[144,512]{1,0:T(8,128)S(1)}, f32[128,128]{1,0:T(8,128)S(1)}, f32[8,128]{1,0:T(8,128)S(1)}) custom-call(bf16[8,16,640]{2,1,0:T(8,128)(2,1)S(1)} %all_to_all.27.all_ref, bf16[144,512]{1,0:T(8,128)(2,1)S(1)} %get-tuple-element.22.cin_ref, bf16[512,512]{1,0:T(8,128)(2,1)S(1)} %copy-done.3, ...), custom_call_target="tpu_custom_call" | custom-call | tf_op jit(solution)/shard_map/step/pallas_call | solution.py:409
  62.4 8.4 %all-to-all-start.4 = ((bf16[16,8,1152]{2,1,0:T(8,128)(2,1)}), bf16[16,8,1152]{2,1,0:T(8,128)(2,1)S(1)}, u32[]{:S(2)}, u32[]{:S(2)}) async-start(bf16[16,8,1152]{2,1,0:T(8,128)(2,1)} %get-tuple-element.24), calls=%async_computation.4 | async-start | bytes 589824 | tf_op jit(solution)/shard_map/all_to_all | solution.py:425
  70.8 3.5 %scan.1 = (f32[128,512]{1,0:T(8,128)S(1)}, f32[128,512]{1,0:T(8,128)S(1)}, bf16[8,128,512]{2,1,0:T(8,128)(2,1)S(1)}, bf16[8,16,512]{2,1,0:T(8,128)(2,1)S(1)}, f32[8,512]{1,0:T(8,128)S(1)}) custom-call(f32[144,512]{1,0:T(8,128)S(1)} %get-tuple-element.25.step_ref, f32[128,128]{1,0:T(8,128)S(1)} %get-tuple-element.26.bc_ref, ...), custom_call_target="tpu_custom_call" | custom-call | tf_op jit(solution)/shard_map/scan/pallas_call | solution.py:426
  74.3 5.7 %all-to-all-done.4.got_ref = bf16[16,8,1152]{2,1,0:T(8,128)(2,1)S(1)} async-done(((bf16[16,8,1152]{2,1,0:T(8,128)(2,1)}), bf16[16,8,1152]{2,1,0:T(8,128)(2,1)S(1)}, u32[]{:S(2)}, u32[]{:S(2)}) %all-to-all-start.4) | async-done | bytes 294944 | tf_op jit(solution)/shard_map/all_to_all | solution.py:425
  80.0 1.6 %finish.1 = (bf16[128,512]{1,0:T(8,128)(2,1)}, bf16[4,2,512]{2,1,0:T(2,128)(2,1)}) custom-call(bf16[16,8,1152]{2,1,0:T(8,128)(2,1)S(1)} %all-to-all-done.4.got_ref, f32[128,512]{1,0:T(8,128)S(1)} %get-tuple-element.29.y_ref, f32[128,512]{1,0:T(8,128)S(1)} %get-tuple-element.30.reach_ref, bf16[8,128,512]{2,1,0:T(8,128)(2,1)S(1)} %get-tuple-element.31.carry_ref, ...), custom_call_target="tpu_custom_call" | custom-call | tf_op jit(solution)/shard_map/finish/pallas_call | solution.py:439
  (18 shorter events, 0.1 us)
Async XLA Ops:
  0.6 11.8 %copy-start.2 = (bf16[128,512]{1,0:T(8,128)(2,1)S(1)}, bf16[128,512]{1,0:T(8,128)(2,1)}, u32[]{:S(2)}) copy-start(bf16[128,512]{1,0:T(8,128)(2,1)} %x_ref.3) | copy-start | bytes 393220
  2.1 10.4 %copy-start.5 = (f32[512,16]{0,1:T(8,128)S(1)}, f32[512,16]{0,1:T(8,128)}, u32[]{:S(2)}) copy-start(f32[512,16]{0,1:T(8,128)} %param.19) | copy-start | bytes 98308
  2.1 10.4 %copy-start.6 = (bf16[4,2,512]{2,1,0:T(2,128)(2,1)S(1)}, bf16[4,2,512]{2,1,0:T(2,128)(2,1)}, u32[]{:S(2)}) copy-start(bf16[4,2,512]{2,1,0:T(2,128)(2,1)} %dz_ref.1) | copy-start | bytes 24580
  2.1 10.4 %copy-start.8 = (bf16[4,512]{1,0:T(4,128)(2,1)S(1)}, bf16[4,512]{1,0:T(4,128)(2,1)}, u32[]{:S(2)}) copy-start(bf16[4,512]{1,0:T(4,128)(2,1)} %w_ref.1) | copy-start | bytes 12292
  2.1 10.4 %copy-start.10 = (f32[512]{0:T(512)S(1)}, f32[512]{0:T(512)}, u32[]{:S(2)}) copy-start(f32[512]{0:T(512)} %skip_ref.1) | copy-start | bytes 6148
  2.1 17.7 %all-to-all-start = ((bf16[16,3,512]{2,1,0:T(4,128)(2,1)}), bf16[16,3,512]{2,1,0:T(4,128)(2,1)S(1)}, u32[]{:S(2)}, u32[]{:S(2)}) async-start(bf16[16,3,512]{2,1,0:T(4,128)(2,1)} %broadcast_in_dim.2), calls=%async_computation | async-start | bytes 131072 | tf_op jit(solution)/shard_map/all_to_all | solution.py:365
  12.4 0.7 copy-start.9
  12.4 0.7 copy-start.11
  12.4 0.7 copy-start.12
  13.1 1.1 %copy-start = (bf16[512,544]{0,1:T(8,128)(2,1)S(1)}, bf16[512,544]{0,1:T(8,128)(2,1)}, u32[]{:S(2)}) copy-start(bf16[512,544]{0,1:T(8,128)(2,1)} %param.16) | copy-start | bytes 1671172
  14.1 0.9 %copy-start.4 = (bf16[128,512]{1,0:T(8,128)(2,1)S(1)}, bf16[128,512]{1,0:T(8,128)(2,1)}, u32[]{:S(2)}) copy-start(bf16[128,512]{1,0:T(8,128)(2,1)} %z_ref.1) | copy-start | bytes 393220
  15.0 4.8 %copy-start.1 = (bf16[512,544]{0,1:T(8,128)(2,1)S(1)}, bf16[512,544]{0,1:T(8,128)(2,1)}, u32[]{:S(2)}) copy-start(bf16[512,544]{0,1:T(8,128)(2,1)} %param.16) | copy-start | bytes 1671172
  15.0 4.8 %copy-start.7 = (bf16[4,2,512]{2,1,0:T(2,128)(2,1)S(1)}, bf16[4,2,512]{2,1,0:T(2,128)(2,1)}, u32[]{:S(2)}) copy-start(bf16[4,2,512]{2,1,0:T(2,128)(2,1)} %dx_ref.1) | copy-start | bytes 24580
  30.3 29.9 %copy-start.3 = (bf16[512,512]{1,0:T(8,128)(2,1)S(1)}, bf16[512,512]{1,0:T(8,128)(2,1)}, u32[]{:S(2)}) copy-start(bf16[512,512]{1,0:T(8,128)(2,1)} %dtw_ref.1) | copy-start | bytes 1572868
  62.4 17.6 %all-to-all-start.4 = ((bf16[16,8,1152]{2,1,0:T(8,128)(2,1)}), bf16[16,8,1152]{2,1,0:T(8,128)(2,1)S(1)}, u32[]{:S(2)}, u32[]{:S(2)}) async-start(bf16[16,8,1152]{2,1,0:T(8,128)(2,1)} %get-tuple-element.24), calls=%async_computation.4 | async-start | bytes 589824 | tf_op jit(solution)/shard_map/all_to_all | solution.py:425

commit v7 on v4

--- a/solution.py
+++ b/solution.py
@@ -162,27 +162,17 @@
 
 def step_kernel(
     all_ref, cin_ref, dtw_ref, small_ref, nrate_ref,
-    msg_ref, step_ref, bc_ref, u_ref, dbc_ref, low_ref, left_ref,
+    msg_ref, step_ref, bc_ref, u_ref, low_ref, left_ref,
 ):
     rows, width = u_ref.shape
-    lines, tiles = [], []
     for k in range(NEAR):
         at = slice(16 * k, 16 * k + 16)
-        tile = all_ref[k, :, R:].astype(F32)
         low_ref[at, :] = all_ref[k, :, :R]
-        bc_ref[at, :] = joined(tile)
-        line, tile = unfolded(tile)
-        lines.append(line)
-        tiles.append(tile)
-    low_ref[rows : rows + 16, :] = jnp.concatenate(
-        lines + [jnp.zeros((8, width), F32)], 0
-    ).astype(BF16)
-    dbc_ref[...] = joined(jnp.concatenate(tiles, 0))
+        bc_ref[at, :] = joined(all_ref[k, :, R:].astype(F32))
     step = softplus(
         jnp.dot(low_ref[...], dtw_ref[...], preferred_element_type=F32) + small_ref[0:1, :]
     )
     step_ref[...] = step
-    step = step[:rows]
     u_ref[...] = step * cin_ref[0:rows, :].astype(F32)
     down = lax.broadcasted_iota(jnp.int32, (rows, rows), 0)
     over = lax.broadcasted_iota(jnp.int32, (rows, rows), 1)
@@ -208,7 +198,7 @@
 
 
 def scan_kernel(
-    step_ref, u_ref, bc_ref, cin_ref, gate_ref, small_ref, nrate_ref, dbc_ref,
+    all_ref, dtw_ref, step_ref, u_ref, bc_ref, cin_ref, gate_ref, small_ref, nrate_ref,
     out_ref, reach_ref, from_ref, dout_ref,
 ):
     rows, width = u_ref.shape
@@ -218,7 +208,13 @@
     reach_ref[...] = sum(
         jnp.dot(upto, part, preferred_element_type=F32) for part in parts(step_ref[0:rows, :])
     )
-    dbc = jnp.transpose(jnp.concatenate([dbc_ref[...], jnp.zeros((120, 128), F32)], 0))
+    pairs = [unfolded(all_ref[k, :, R:].astype(F32)) for k in range(NEAR)]
+    low = jnp.concatenate([line for line, _ in pairs] + [jnp.zeros((8, width), F32)], 0)
+    dstep = softplus(
+        jnp.dot(low.astype(BF16), dtw_ref[...], preferred_element_type=F32) + small_ref[0:1, :]
+    )
+    dbc = joined(jnp.concatenate([tile for _, tile in pairs], 0))
+    dbc = jnp.transpose(jnp.concatenate([dbc, jnp.zeros((120, 128), F32)], 0))
     nrate = nrate_ref[...]
     skip = small_ref[1:2, :]
     bct = jnp.transpose(bc_ref[...])[0 : 2 * N]
@@ -243,7 +239,7 @@
     state = [jnp.zeros((N, width), F32) for _ in range(2)]
     for r in range(2 * STEPS):
         s = r % 2
-        d = step_ref[rows + r : rows + r + 1, :]
+        d = dstep[r : r + 1]
         decay = jnp.exp(nrate * d)
         kept[s] = decay * kept[s]
         state[s] = decay * state[s] + dbc[0:N, r : r + 1] * (d * dec[r : r + 1])
@@ -392,16 +388,15 @@
     sums = call(far_sum_kernel, shape(NEAR, 16, WIDE, kind=BF16), inputs=1, name="far_sum")(got)
     everything = lax.all_to_all(sums, "tensor", 0, 0, axis_index_groups=near)
 
-    send, step, bc, u, dbc = call(
+    send, step, bc, u = call(
         step_kernel,
         (
             shape(places, N // 2, 2 * width + 128, kind=BF16),
-            shape(rows + 16, width),
+            shape(rows, width),
             shape(rows, 128),
             shape(rows, width),
-            shape(8, 128),
         ),
-        [pltpu.VMEM((rows + 16, R), BF16), pltpu.VMEM((rows, width), F32)],
+        [pltpu.VMEM((rows, R), BF16), pltpu.VMEM((rows, width), F32)],
         inputs=5,
         name="step",
     )(everything, cin, dtproj_weight, small, nrate)
@@ -414,9 +409,9 @@
             shape(2 * STEPS, N, width),
             shape(2 * STEPS, width),
         ),
-        inputs=8,
+        inputs=9,
         name="scan",
-    )(step, u, bc, cin, gate, small, nrate, dbc)
+    )(everything, dtproj_weight, step, u, bc, cin, gate, small, nrate)
     return call(
         finish_kernel,
         (shape(rows, width, kind=BF16), shape(STEPS, 2, width, kind=BF16)),

time: 82.4 us -> 82.4 us (level)
  transfers between devices with their start and end apart: 2 -> 2, of which waited for: 2 -> 2; matrix products, arithmetic and copies ran while one was open for 0% -> 0% of each run, Pallas kernels for 4% -> 5%
where the time goes in v7:
time: 82.4 us; the launch traced here: 81.9 us
  blocking collectives  39.9 us (48%)
  starting transfers between devices  18.7 us (23%)
  waiting for transfers between devices  10.3 us (12%)
  Pallas kernels  8.22 us (10%)
  local copies, waits for them, and re-layouts  4.03 us (5%)
    all_to_all x1, blocking collectives, local(): got = lax.all_to_all(sums, 'tensor', 0, 0, axis_index_groups=far)  19.3 us
    all_to_all x1, blocking collectives, local(): everything = lax.all_to_all(sums, 'tensor', 0, 0, axis_index_groups=near)  10.4 us
    all_to_all x1, starting transfers between devices, local(): lax.all_to_all(jnp.broadcast_to(tail[None], (places, taps - 1, width)), '...  10.3 us
    all_to_all x1, blocking collectives, local(): got = lax.all_to_all(part, 'tensor', 0, 0, axis_index_groups=near)  10.2 us
    all_to_all x1, starting transfers between devices, local(): states = lax.all_to_all(send, 'group', 0, 0)  8.41 us
    all_to_all x1, waiting for transfers between devices, local(): states = lax.all_to_all(send, 'group', 0, 0)  6.49 us
    all_to_all x1, waiting for transfers between devices, local(): lax.all_to_all(jnp.broadcast_to(tail[None], (places, taps - 1, width)), '...  3.77 us
    pallas_call x1, Pallas kernels, local(): call(scan_kernel, (shape(rows, width), shape(rows, width), shape(2 * STEP...  2.72 us
  transfers between devices with their start and end apart: 2, of which 2 were waited for; matrix products, arithmetic and copies ran while one was open for 0% of the time, Pallas kernels for 5%

profile of v7, /device:TPU:1, one launch (start us, length us, event | category | flops | bytes accessed | tf_op | source)
XLA Modules:
  0.0 81.9 jit_solution(16137800315585312998)
XLA Ops:
  0.6 0.0 copy-start.3
  0.6 0.8 slice.3
  1.4 0.7 broadcast_in_dim.2
  2.1 10.3 %all-to-all-start = ((bf16[16,3,512]{2,1,0:T(4,128)(2,1)}), bf16[16,3,512]{2,1,0:T(4,128)(2,1)S(1)}, u32[]{:S(2)}, u32[]{:S(2)}) async-start(bf16[16,3,512]{2,1,0:T(4,128)(2,1)} %broadcast_in_dim.2), calls=%async_computation | async-start | bytes 131072 | tf_op jit(solution)/shard_map/all_to_all | solution.py:347
  12.4 0.0 copy-start.11
  12.4 0.0 copy-start.12
  12.5 0.6 copy-done.9
  13.1 0.0 copy-done.11
  13.1 1.1 %copy-done = bf16[512,544]{0,1:T(8,128)(2,1)S(1)} copy-done((bf16[512,544]{0,1:T(8,128)(2,1)S(1)}, bf16[512,544]{0,1:T(8,128)(2,1)}, u32[]{:S(2)}) %copy-start) | copy-done | bytes 557080
  14.1 0.9 %copy-done.4 = bf16[128,512]{1,0:T(8,128)(2,1)S(1)} copy-done((bf16[128,512]{1,0:T(8,128)(2,1)S(1)}, bf16[128,512]{1,0:T(8,128)(2,1)}, u32[]{:S(2)}) %copy-start.4) | copy-done | bytes 131096
  15.0 1.0 %prepare.1 = (f32[128,640]{1,0:T(8,128)S(1)}, bf16[128,512]{1,0:T(8,128)(2,1)S(1)}, f32[16,512]{1,0:T(8,128)S(1)}, f32[128,512]{1,0:T(8,128)S(1)}, f32[24,512]{1,0:T(8,128)S(1)}) custom-call(s32[2]{0:T(128)S(1)} %copy-done.12, bf16[128,512]{1,0:T(8,128)(2,1)S(1)} %copy-done.3, bf16[4,512]{1,0:T(4,128)(2,1)S(1)} %copy-done.8, bf16[512]{0:T(512)(128)(2,1)S(1)} %copy-done.11, ...), custom_call_target="tpu_custom_call" | custom-call | tf_op jit(solution)/shard_map/prepare/pallas_call | solution.py:351
  16.0 3.8 %all-to-all-done.tails_ref = bf16[16,3,512]{2,1,0:T(4,128)(2,1)S(1)} async-done(((bf16[16,3,512]{2,1,0:T(4,128)(2,1)}), bf16[16,3,512]{2,1,0:T(4,128)(2,1)S(1)}, u32[]{:S(2)}, u32[]{:S(2)}) %all-to-all-start) | async-done | bytes 49184 | tf_op jit(solution)/shard_map/all_to_all | solution.py:347
  19.8 0.0 copy-done.7
  19.8 0.3 project.1
  20.2 10.2 %all_to_all.25.got_ref = bf16[8,16,640]{2,1,0:T(8,128)(2,1)S(1)} all-to-all(bf16[8,16,640]{2,1,0:T(8,128)(2,1)S(1)} %get-tuple-element.20), channel_id=1, replica_groups={{0,1,2,3,4,5,6,7},{10,11,12,13,14,15,8,9},{20,21,22,23,16,17,18,19},{30..., dimensions={0} | all-to-all | bytes 327680 | tf_op jit(solution)/shard_map/all_to_all | solution.py:383
  30.4 19.3 %all_to_all.26.got_ref = bf16[4,16,640]{2,1,0:T(8,128)(2,1)S(1)} all-to-all(bf16[4,16,640]{2,1,0:T(8,128)(2,1)S(1)} %near_sum.1), channel_id=1, replica_groups={{0,10,20,30},{1,11,21,31},{2,12,22,24},{3,13,23,25},{4,14,16,26},{5,15,..., dimensions={0} | all-to-all | bytes 163840 | tf_op jit(solution)/shard_map/all_to_all | solution.py:387
  49.7 0.1 far_sum.1
  49.8 10.4 %all_to_all.27.all_ref = bf16[8,16,640]{2,1,0:T(8,128)(2,1)S(1)} all-to-all(bf16[8,16,640]{2,1,0:T(8,128)(2,1)S(1)} %far_sum.1), channel_id=1, replica_groups={{0,1,2,3,4,5,6,7},{10,11,12,13,14,15,8,9},{20,21,22,23,16,17,18,19},{30..., dimensions={0} | all-to-all | bytes 327680 | tf_op jit(solution)/shard_map/all_to_all | solution.py:389
  60.2 0.0 copy-done.2
  60.2 2.3 %step.1 = (bf16[16,8,1152]{2,1,0:T(8,128)(2,1)}, f32[128,512]{1,0:T(8,128)S(1)}, f32[128,128]{1,0:T(8,128)S(1)}, f32[128,512]{1,0:T(8,128)S(1)}) custom-call(bf16[8,16,640]{2,1,0:T(8,128)(2,1)S(1)} %all_to_all.27.all_ref, bf16[144,512]{1,0:T(8,128)(2,1)S(1)} %get-tuple-element.21.cin_ref, bf16[512,512]{1,0:T(8,128)(2,1)S(1)} %copy-done.2, ...), custom_call_target="tpu_custom_call" | custom-call | tf_op jit(solution)/shard_map/step/pallas_call | solution.py:391
  62.5 8.4 %all-to-all-start.4 = ((bf16[16,8,1152]{2,1,0:T(8,128)(2,1)}), bf16[16,8,1152]{2,1,0:T(8,128)(2,1)S(1)}, u32[]{:S(2)}, u32[]{:S(2)}) async-start(bf16[16,8,1152]{2,1,0:T(8,128)(2,1)} %get-tuple-element.23), calls=%async_computation.4 | async-start | bytes 589824 | tf_op jit(solution)/shard_map/all_to_all | solution.py:403
  70.9 2.7 %scan.1 = (f32[128,512]{1,0:T(8,128)S(1)}, f32[128,512]{1,0:T(8,128)S(1)}, f32[8,16,512]{2,1,0:T(8,128)S(1)}, f32[8,512]{1,0:T(8,128)S(1)}) custom-call(bf16[8,16,640]{2,1,0:T(8,128)(2,1)S(1)} %all_to_all.27.all_ref, bf16[512,512]{1,0:T(8,128)(2,1)S(1)} %copy-done.2, f32[128,512]{1,0:T(8,128)S(1)} %get-tuple-element.24.step_ref, ...), custom_call_target="tpu_custom_call" | custom-call | tf_op jit(solution)/shard_map/scan/pallas_call | solution.py:404
  73.6 6.5 %all-to-all-done.4.got_ref = bf16[16,8,1152]{2,1,0:T(8,128)(2,1)S(1)} async-done(((bf16[16,8,1152]{2,1,0:T(8,128)(2,1)}), bf16[16,8,1152]{2,1,0:T(8,128)(2,1)S(1)}, u32[]{:S(2)}, u32[]{:S(2)}) %all-to-all-start.4) | async-done | bytes 294944 | tf_op jit(solution)/shard_map/all_to_all | solution.py:403
  80.1 1.8 %finish.1 = (bf16[128,512]{1,0:T(8,128)(2,1)}, bf16[4,2,512]{2,1,0:T(2,128)(2,1)}) custom-call(bf16[16,8,1152]{2,1,0:T(8,128)(2,1)S(1)} %all-to-all-done.4.got_ref, f32[128,512]{1,0:T(8,128)S(1)} %get-tuple-element.28.y_ref, f32[128,512]{1,0:T(8,128)S(1)} %get-tuple-element.29.reach_ref, f32[128,128]{1,0:T(8,128)S(1)} %get-tuple-element.26.bc_ref, ...), custom_call_target="tpu_custom_call" | custom-call | tf_op jit(solution)/shard_map/finish/pallas_call | solution.py:415
  (18 shorter events, 0.1 us)
Async XLA Ops:
  0.6 11.8 %copy-start.3 = (bf16[128,512]{1,0:T(8,128)(2,1)S(1)}, bf16[128,512]{1,0:T(8,128)(2,1)}, u32[]{:S(2)}) copy-start(bf16[128,512]{1,0:T(8,128)(2,1)} %x_ref.3) | copy-start | bytes 393220
  2.1 10.4 %copy-start.5 = (f32[512,16]{0,1:T(8,128)S(1)}, f32[512,16]{0,1:T(8,128)}, u32[]{:S(2)}) copy-start(f32[512,16]{0,1:T(8,128)} %param.19) | copy-start | bytes 98308
  2.1 10.4 %copy-start.6 = (bf16[4,2,512]{2,1,0:T(2,128)(2,1)S(1)}, bf16[4,2,512]{2,1,0:T(2,128)(2,1)}, u32[]{:S(2)}) copy-start(bf16[4,2,512]{2,1,0:T(2,128)(2,1)} %dz_ref.1) | copy-start | bytes 24580
  2.1 10.4 %copy-start.8 = (bf16[4,512]{1,0:T(4,128)(2,1)S(1)}, bf16[4,512]{1,0:T(4,128)(2,1)}, u32[]{:S(2)}) copy-start(bf16[4,512]{1,0:T(4,128)(2,1)} %w_ref.1) | copy-start | bytes 12292
  2.1 10.4 %copy-start.10 = (f32[512]{0:T(512)S(1)}, f32[512]{0:T(512)}, u32[]{:S(2)}) copy-start(f32[512]{0:T(512)} %skip_ref.1) | copy-start | bytes 6148
  2.1 17.7 %all-to-all-start = ((bf16[16,3,512]{2,1,0:T(4,128)(2,1)}), bf16[16,3,512]{2,1,0:T(4,128)(2,1)S(1)}, u32[]{:S(2)}, u32[]{:S(2)}) async-start(bf16[16,3,512]{2,1,0:T(4,128)(2,1)} %broadcast_in_dim.2), calls=%async_computation | async-start | bytes 131072 | tf_op jit(solution)/shard_map/all_to_all | solution.py:347
  12.4 0.7 copy-start.9
  12.4 0.7 copy-start.11
  12.4 0.7 copy-start.12
  13.1 1.1 %copy-start = (bf16[512,544]{0,1:T(8,128)(2,1)S(1)}, bf16[512,544]{0,1:T(8,128)(2,1)}, u32[]{:S(2)}) copy-start(bf16[512,544]{0,1:T(8,128)(2,1)} %param.16) | copy-start | bytes 1671172
  14.1 0.9 %copy-start.4 = (bf16[128,512]{1,0:T(8,128)(2,1)S(1)}, bf16[128,512]{1,0:T(8,128)(2,1)}, u32[]{:S(2)}) copy-start(bf16[128,512]{1,0:T(8,128)(2,1)} %z_ref.1) | copy-start | bytes 393220
  15.0 4.8 %copy-start.1 = (bf16[512,544]{0,1:T(8,128)(2,1)S(1)}, bf16[512,544]{0,1:T(8,128)(2,1)}, u32[]{:S(2)}) copy-start(bf16[512,544]{0,1:T(8,128)(2,1)} %param.16) | copy-start | bytes 1671172
  15.0 4.8 %copy-start.7 = (bf16[4,2,512]{2,1,0:T(2,128)(2,1)S(1)}, bf16[4,2,512]{2,1,0:T(2,128)(2,1)}, u32[]{:S(2)}) copy-start(bf16[4,2,512]{2,1,0:T(2,128)(2,1)} %dx_ref.1) | copy-start | bytes 24580
  30.3 29.9 %copy-start.2 = (bf16[512,512]{1,0:T(8,128)(2,1)S(1)}, bf16[512,512]{1,0:T(8,128)(2,1)}, u32[]{:S(2)}) copy-start(bf16[512,512]{1,0:T(8,128)(2,1)} %dtw_ref.3) | copy-start | bytes 1572868
  62.5 17.6 %all-to-all-start.4 = ((bf16[16,8,1152]{2,1,0:T(8,128)(2,1)}), bf16[16,8,1152]{2,1,0:T(8,128)(2,1)S(1)}, u32[]{:S(2)}, u32[]{:S(2)}) async-start(bf16[16,8,1152]{2,1,0:T(8,128)(2,1)} %get-tuple-element.23), calls=%async_computation.4 | async-start | bytes 589824 | tf_op jit(solution)/shard_map/all_to_all | solution.py:403
